TPU v7x, 128 devices: a whole 4x4x4 slice. The times are simulated.
128 devices in a mesh: dp: 32 (over y, x, core), section: 4 (over z).
Axes of the slice: x: 4, y: 4, z: 4, core: 2. Of those that a mesh axis runs over, the one named last changes fastest.
Arguments:
- inputs: bfloat16 [256, 128, 200], P('dp'), may hold values from -6 to 6
- lengths: int32 [256], P('dp'), may hold values from 1 to 128, as said below
- gene_mask: int32 [256, 128], P('dp'), may hold values from 0 to 1, as said below
- out_grad: float32 [256, 128, 200], P('dp'), may hold values from -6 to 6
- norm_gain: float32 [2, 2, 200], replicated, may hold values from 0.5 to 1.5
- norm_bias: float32 [2, 2, 200], replicated, may hold values from -1.75 to 1.75
- qkv_weight: bfloat16 [2, 200, 1920], replicated, may hold values from -0.3125 to 0.3125
- out_weight: bfloat16 [2, 640, 200], replicated, may hold values from -0.625 to 0.625
- out_bias: float32 [2, 200], replicated, may hold values from -1.75 to 1.75
- features: bfloat16 [2, 64, 266], replicated, may hold values from -6 to 6
- up_weight: bfloat16 [2, 200, 800], replicated, may hold values from -0.4375 to 0.4375
- up_bias: float32 [2, 800], replicated, may hold values from -1.75 to 1.75
- down_weight: bfloat16 [2, 800, 200], replicated, may hold values from -0.3125 to 0.3125
- down_bias: float32 [2, 200], replicated, may hold values from -1.75 to 1.75
Outputs:
- activations: float32 [4, 256, 128, 200], P('section', 'dp')
- stream_grads: float32 [4, 256, 128, 200], P('section', 'dp')
- grad_norm_gain: float32 [2, 2, 200], replicated
- grad_norm_bias: float32 [2, 2, 200], replicated
- grad_qkv_weight: float32 [2, 200, 1920], replicated
- grad_out_weight: float32 [2, 640, 200], replicated
- grad_out_bias: float32 [2, 200], replicated
- grad_up_weight: float32 [2, 200, 800], replicated
- grad_up_bias: float32 [2, 800], replicated
- grad_down_weight: float32 [2, 800, 200], replicated
- grad_down_bias: float32 [2, 200], replicated
Inputs may be any that keep to these rules, and one draw needn't show every extreme that they name: `lengths`: some cell has exactly 128 expressed genes. `gene_mask`: the first slot of every cell is 1.
All inputs are finite; a program needn't handle non-finite values.
Results may differ from a plain program's by a relative error of at most 0.029.
Values sent between devices are 32-bit elements; how exact they have to be, the bound alone decides.
A program may use at most 192 MiB of HBM per device.

v0:
```python
from functools import partial

import jax
import jax.numpy as jnp
from jax import lax
from jax.sharding import PartitionSpec as P

HEADS = 10
HEAD_DIM = 64
FEATS = 266
FF = 800
MICRO = 2


EPSILON = 1e-05
ACCURATE = lax.Precision.HIGHEST


def from_behind(value, axis, by):
    length = lax.axis_size(axis)
    pairs = [(i, i + by) for i in range(length) if 0 <= i + by < length]
    return lax.ppermute(value, axis, pairs)


def flat_size(widths, inner_width):
    return max(4 * widths * inner_width, 2 * widths * FF)


def pad_flat(first, second, total):
    joined = jnp.concatenate([first.reshape(-1), second.reshape(-1)])
    return jnp.pad(joined, (0, total - joined.shape[0]))


def layer_norm(rows, gain_row, shift_row):
    centered = rows - jnp.mean(rows, axis=-1, keepdims=True)
    inverse = lax.rsqrt(jnp.mean(centered * centered, axis=-1, keepdims=True) + EPSILON)
    normed = centered * inverse
    return ((normed * gain_row + shift_row).astype(jnp.bfloat16), normed, inverse)


def norm_backward(grad_normed, normed, inverse, gain_row):
    gain_grad = jnp.sum(grad_normed * normed, axis=0)
    shift_grad = jnp.sum(grad_normed, axis=0)
    scaled = grad_normed * gain_row
    grad_in = inverse * (
        scaled
        - jnp.mean(scaled, axis=-1, keepdims=True)
        - normed * jnp.mean(scaled * normed, axis=-1, keepdims=True)
    )
    return (grad_in, gain_grad, shift_grad)


def feature_logits(vectors, random_map):
    product = jnp.einsum("cnhe,ef->cnhf", vectors, random_map, preferred_element_type=jnp.float32)
    squares = jnp.sum(jnp.square(vectors.astype(jnp.float32)), axis=-1, keepdims=True)
    return product * HEAD_DIM ** (-0.25) - squares * (0.5 * HEAD_DIM ** (-0.5))


def logit_backward(grad_logit, vectors, random_map):
    spread = jnp.einsum("cnhf,ef->cnhe", grad_logit, random_map, preferred_element_type=jnp.float32)
    totals = jnp.sum(grad_logit, axis=-1, keepdims=True, dtype=jnp.float32)
    return spread * HEAD_DIM ** (-0.25) - totals * HEAD_DIM ** (-0.5) * vectors.astype(jnp.float32)


def attend_forward(stream, key_mask, weights):
    gain_row, shift_row, qkv_mats, out_mats, out_shift, random_map = weights
    cell_count, slot_count, widths = stream.shape
    inner_width = out_mats.shape[0]
    normed_low, normed, inverse = layer_norm(stream.reshape(-1, widths), gain_row, shift_row)
    projected = jnp.dot(normed_low, qkv_mats, preferred_element_type=jnp.float32).astype(
        jnp.bfloat16
    )
    shaped = projected.reshape(cell_count, slot_count, 3, HEADS, inner_width // HEADS)
    query, keys, values = (shaped[:, :, 0], shaped[:, :, 1], shaped[:, :, 2])
    query_logit = feature_logits(query, random_map)
    key_logit = feature_logits(keys, random_map)
    query_feat = (jnp.exp(query_logit) * FEATS ** (-0.5)).astype(jnp.bfloat16)
    key_feat = (jnp.exp(key_logit) * FEATS ** (-0.5)).astype(jnp.bfloat16) * key_mask[
        :, :, None, None
    ]
    key_value = jnp.einsum(
        "cnhf,cnhe->chfe", key_feat, values, preferred_element_type=jnp.float32
    ).astype(jnp.bfloat16)
    key_total = jnp.sum(key_feat, axis=1, dtype=jnp.float32)
    numerator = jnp.einsum(
        "cnhf,chfe->cnhe", query_feat, key_value, preferred_element_type=jnp.float32
    )
    denominator = jnp.einsum(
        "cnhf,chf->cnh", query_feat.astype(jnp.float32), key_total, precision=ACCURATE
    )
    attended = (numerator / denominator[..., None]).reshape(-1, inner_width).astype(jnp.bfloat16)
    branch = jnp.dot(attended, out_mats, preferred_element_type=jnp.float32) + out_shift
    saved = (
        normed_low,
        normed,
        inverse,
        query,
        keys,
        values,
        query_logit,
        key_logit,
        query_feat,
        key_feat,
        key_value,
        key_total,
        numerator,
        denominator,
        attended,
    )
    return (stream + branch.reshape(stream.shape), saved)


def attend_backward(stream, key_mask, weights, incoming):
    gain_row, shift_row, qkv_mats, out_mats, out_shift, random_map = weights
    widths = stream.shape[2]
    inner_width = out_mats.shape[0]
    result, saved = attend_forward(stream, key_mask, weights)
    (
        normed_low,
        normed,
        inverse,
        query,
        keys,
        values,
        query_logit,
        key_logit,
        query_feat,
        key_feat,
        key_value,
        key_total,
        numerator,
        denominator,
        attended,
    ) = saved
    grad_low = incoming.reshape(-1, widths).astype(jnp.bfloat16)
    out_mat_grad = jnp.einsum("rd,re->de", attended, grad_low, preferred_element_type=jnp.float32)
    out_shift_grad = jnp.sum(grad_low, axis=0, dtype=jnp.float32)
    grad_att = jnp.einsum(
        "re,de->rd", grad_low, out_mats, preferred_element_type=jnp.float32
    ).reshape(numerator.shape)
    grad_num = (grad_att / denominator[..., None]).astype(jnp.bfloat16)
    grad_den = (-jnp.sum(grad_att * numerator, axis=-1) / (denominator * denominator)).astype(
        jnp.bfloat16
    )
    grad_qfeat = (
        jnp.einsum("cnhe,chfe->cnhf", grad_num, key_value, preferred_element_type=jnp.float32)
        + grad_den.astype(jnp.float32)[..., None] * key_total[:, None]
    )
    grad_kv = jnp.einsum(
        "cnhf,cnhe->chfe", query_feat, grad_num, preferred_element_type=jnp.float32
    ).astype(jnp.bfloat16)
    grad_ktotal = jnp.einsum(
        "cnhf,cnh->chf", query_feat, grad_den, preferred_element_type=jnp.float32
    )
    grad_kfeat = (
        jnp.einsum("cnhe,chfe->cnhf", values, grad_kv, preferred_element_type=jnp.float32)
        + grad_ktotal[:, None]
    ) * key_mask.astype(jnp.float32)[:, :, None, None]
    grad_values = jnp.einsum(
        "cnhf,chfe->cnhe", key_feat, grad_kv, preferred_element_type=jnp.float32
    )
    grad_qlogit = (grad_qfeat * jnp.exp(query_logit) * FEATS ** (-0.5)).astype(jnp.bfloat16)
    grad_klogit = (grad_kfeat * jnp.exp(key_logit) * FEATS ** (-0.5)).astype(jnp.bfloat16)
    grad_query = logit_backward(grad_qlogit, query, random_map)
    grad_keys = logit_backward(grad_klogit, keys, random_map)
    grad_proj = (
        jnp.stack([grad_query, grad_keys, grad_values], axis=2)
        .reshape(-1, 3 * inner_width)
        .astype(jnp.bfloat16)
    )
    qkv_grad = jnp.einsum("rd,rk->dk", normed_low, grad_proj, preferred_element_type=jnp.float32)
    grad_normed = jnp.einsum("rk,dk->rd", grad_proj, qkv_mats, preferred_element_type=jnp.float32)
    grad_in, gain_grad, shift_grad = norm_backward(grad_normed, normed, inverse, gain_row)
    flat_grad = pad_flat(qkv_grad, out_mat_grad, flat_size(widths, inner_width))
    terms = (gain_grad, shift_grad, flat_grad, jnp.zeros((FF,), jnp.float32), out_shift_grad)
    return (incoming + grad_in.reshape(stream.shape), terms)


def mix_forward(stream, weights):
    gain_row, shift_row, up_mats, up_shift, down_mats, down_shift = weights
    widths = stream.shape[2]
    normed_low, normed, inverse = layer_norm(stream.reshape(-1, widths), gain_row, shift_row)
    before = jnp.dot(normed_low, up_mats, preferred_element_type=jnp.float32) + up_shift
    hidden = jax.nn.gelu(before, approximate=False).astype(jnp.bfloat16)
    branch = jnp.dot(hidden, down_mats, preferred_element_type=jnp.float32) + down_shift
    return (stream + branch.reshape(stream.shape), (normed_low, normed, inverse, before, hidden))


def mix_backward(stream, weights, incoming, inner_width):
    gain_row, shift_row, up_mats, up_shift, down_mats, down_shift = weights
    widths = stream.shape[2]
    result, saved = mix_forward(stream, weights)
    normed_low, normed, inverse, before, hidden = saved
    grad_low = incoming.reshape(-1, widths).astype(jnp.bfloat16)
    down_grad = jnp.einsum("rf,rd->fd", hidden, grad_low, preferred_element_type=jnp.float32)
    down_shift_grad = jnp.sum(grad_low, axis=0, dtype=jnp.float32)
    grad_hidden = jnp.einsum("rd,fd->rf", grad_low, down_mats, preferred_element_type=jnp.float32)
    gelu_pull = jax.vjp(partial(jax.nn.gelu, approximate=False), before)[1]
    grad_before = gelu_pull(grad_hidden)[0].astype(jnp.bfloat16)
    up_grad = jnp.einsum("rd,rf->df", normed_low, grad_before, preferred_element_type=jnp.float32)
    up_shift_grad = jnp.sum(grad_before, axis=0, dtype=jnp.float32)
    grad_normed = jnp.einsum("rf,df->rd", grad_before, up_mats, preferred_element_type=jnp.float32)
    grad_in, gain_grad, shift_grad = norm_backward(grad_normed, normed, inverse, gain_row)
    flat_grad = pad_flat(up_grad, down_grad, flat_size(widths, inner_width))
    terms = (gain_grad, shift_grad, flat_grad, up_shift_grad, down_shift_grad)
    return (incoming + grad_in.reshape(stream.shape), terms)


def body(
    inputs,
    lengths,
    gene_mask,
    out_grad,
    norm_gain,
    norm_bias,
    qkv_weight,
    out_weight,
    out_bias,
    features,
    up_weight,
    up_bias,
    down_weight,
    down_bias,
):
    section_count = lax.axis_size("section")
    section_index = lax.axis_index("section")
    layer_index = section_index // 2
    is_mix = section_index % 2 == 1
    layer_count = norm_gain.shape[0]
    cell_count, slot_count, widths = inputs.shape
    inner_width = out_weight.shape[1]
    total_flat = flat_size(widths, inner_width)
    per_micro = cell_count // MICRO
    ticks = MICRO + section_count - 1

    def select(stacked):
        return lax.dynamic_index_in_dim(stacked, layer_index, 0, keepdims=False)

    gain_pair = select(norm_gain)
    shift_pair = select(norm_bias)
    attend_weights = (
        gain_pair[0],
        shift_pair[0],
        select(qkv_weight),
        select(out_weight),
        select(out_bias),
        select(features),
    )
    mix_weights = (
        gain_pair[1],
        shift_pair[1],
        select(up_weight),
        select(up_bias),
        select(down_weight),
        select(down_bias),
    )
    positions = lax.broadcasted_iota(jnp.int32, (cell_count, slot_count), 1)
    key_mask = jnp.where((positions < lengths[:, None]) & (gene_mask > 0), 1.0, 0.0).astype(
        jnp.bfloat16
    )
    kept = jnp.zeros((cell_count, slot_count, widths), jnp.float32)
    states = jnp.zeros((cell_count, slot_count, widths), jnp.float32)
    arrived = jnp.zeros((per_micro, slot_count, widths), jnp.float32)
    for step_index in range(ticks):
        micro_index = step_index - section_index
        live = (micro_index >= 0) & (micro_index < MICRO)
        start = jnp.clip(micro_index, 0, MICRO - 1) * per_micro
        entry_micro = min(step_index, MICRO - 1)
        entering = inputs[entry_micro * per_micro : (entry_micro + 1) * per_micro].astype(
            jnp.float32
        )
        stream = jnp.where(section_index == 0, entering, arrived)
        masks = lax.dynamic_slice_in_dim(key_mask, start, per_micro, 0)
        result = lax.cond(
            is_mix,
            lambda moving, marks: mix_forward(moving, mix_weights)[0],
            lambda moving, marks: attend_forward(moving, marks, attend_weights)[0],
            stream,
            masks,
        )
        kept = jnp.where(live, lax.dynamic_update_slice_in_dim(kept, stream, start, 0), kept)
        states = jnp.where(live, lax.dynamic_update_slice_in_dim(states, result, start, 0), states)
        if step_index + 1 < ticks:
            arrived = from_behind(result, "section", 1)
    grads = (
        jnp.zeros((widths,), jnp.float32),
        jnp.zeros((widths,), jnp.float32),
        jnp.zeros((total_flat,), jnp.float32),
        jnp.zeros((FF,), jnp.float32),
        jnp.zeros((widths,), jnp.float32),
    )
    stream_grads = jnp.zeros((cell_count, slot_count, widths), jnp.float32)
    arrived = jnp.zeros((per_micro, slot_count, widths), jnp.float32)
    for step_index in range(ticks):
        micro_index = step_index - (section_count - 1 - section_index)
        live = (micro_index >= 0) & (micro_index < MICRO)
        start = jnp.clip(micro_index, 0, MICRO - 1) * per_micro
        entry_micro = min(step_index, MICRO - 1)
        entering = out_grad[entry_micro * per_micro : (entry_micro + 1) * per_micro]
        incoming = jnp.where(section_index == section_count - 1, entering, arrived)
        stream = lax.dynamic_slice_in_dim(kept, start, per_micro, 0)
        masks = lax.dynamic_slice_in_dim(key_mask, start, per_micro, 0)
        passed, terms = lax.cond(
            is_mix,
            lambda moving, marks, grads_in: mix_backward(
                moving, mix_weights, grads_in, inner_width
            ),
            lambda moving, marks, grads_in: attend_backward(
                moving, marks, attend_weights, grads_in
            ),
            stream,
            masks,
            incoming,
        )
        grads = tuple((total + jnp.where(live, term, 0.0) for total, term in zip(grads, terms)))
        stream_grads = jnp.where(
            live, lax.dynamic_update_slice_in_dim(stream_grads, passed, start, 0), stream_grads
        )
        if step_index + 1 < ticks:
            arrived = from_behind(passed, "section", -1)
    gain_grad, shift_grad, flat_grad, up_shift_grad, shift_out_grad = grads
    qkv_count = 3 * widths * inner_width
    out_count = inner_width * widths
    up_count = widths * FF
    layer_hot = (jnp.arange(layer_count) == layer_index).astype(jnp.float32)
    kind_hot = (jnp.arange(2) == section_index % 2).astype(jnp.float32)
    slot_hot = layer_hot[:, None] * kind_hot[None, :]
    attend_hot = layer_hot * kind_hot[0]
    mix_hot = layer_hot * kind_hot[1]
    summed = lax.psum(
        (
            slot_hot[..., None] * gain_grad,
            slot_hot[..., None] * shift_grad,
            attend_hot[:, None] * flat_grad,
            mix_hot[:, None] * flat_grad,
            attend_hot[:, None] * shift_out_grad,
            mix_hot[:, None] * up_shift_grad,
            mix_hot[:, None] * shift_out_grad,
        ),
        ("dp", "section"),
    )
    (
        gain_total,
        shift_total,
        attend_flat,
        mix_flat,
        out_shift_total,
        up_shift_total,
        down_shift_total,
    ) = summed
    qkv_total = attend_flat[:, :qkv_count].reshape(layer_count, widths, 3 * inner_width)
    out_total = attend_flat[:, qkv_count : qkv_count + out_count].reshape(
        layer_count, inner_width, widths
    )
    up_total = mix_flat[:, :up_count].reshape(layer_count, widths, FF)
    down_total = mix_flat[:, up_count : 2 * up_count].reshape(layer_count, FF, widths)
    return (
        states[None],
        stream_grads[None],
        gain_total,
        shift_total,
        qkv_total,
        out_total,
        out_shift_total,
        up_total,
        up_shift_total,
        down_total,
        down_shift_total,
    )


def solution(mesh):
    placed = (
        P("dp", None, None),
        P("dp"),
        P("dp", None),
        P("dp", None, None),
        P(),
        P(),
        P(),
        P(),
        P(),
        P(),
        P(),
        P(),
        P(),
        P(),
    )
    return jax.shard_map(
        body,
        mesh=mesh,
        in_specs=placed,
        out_specs=(
            P("section", "dp", None, None),
            P("section", "dp", None, None),
            P(),
            P(),
            P(),
            P(),
            P(),
            P(),
            P(),
            P(),
            P(),
        ),
        check_vma=False,
    )
```

profile of v0, /device:TPU:1, one launch (start us, length us, event | category | flops | bytes accessed | tf_op | source)
XLA Modules:
  0.0 771.2 jit_solution(6822778667208986748)
XLA Ops:
  14.3 29.2 %conditional.10 = (f32[4,128,200]{1,2,0:T(8,128)S(1)}) conditional(s32[]{:T(128)} %convert_element_type.954, (f32[4,128,200]{1,2,0:T(8,128)S(1)}, f32[1,200]{1,0:T(1,128)S(1)}, f32[1,200]{1,0:T(1,128)S(1)}, bf16[200,1920]{1,0:T(8,128)(2,1)S(1)}, bf16[64,266]{1,0:T(8,128)(2,1)S(1)}, /*index=5*/bf16[8,128]{1,0:T(8,128)(2,1)S(1)}, s32[]{:T(128)}, ...), branch_computations={%region_0.6_spmd, %region_6.9_spmd} | conditional | flops 1258316928 | bytes 50129932 | solution.py:274
  20.7 4.4 reshape.1428
  35.4 4.8 divide_convert_fusion
  44.8 7.6 collective-permute-done
  53.2 40.9 %conditional.11 = (f32[4,128,200]{1,2,0:T(8,128)}) conditional(s32[]{:T(128)} %convert_element_type.954, (f32[4,128,200]{1,2,0:T(8,128)S(1)}, f32[1,200]{1,0:T(1,128)S(1)}, f32[1,200]{1,0:T(1,128)S(1)}, bf16[200,1920]{1,0:T(8,128)(2,1)S(1)}, bf16[64,266]{1,0:T(8,128)(2,1)S(1)}, /*index=5*/bf16[8,128]{1,0:T(8,128)(2,1)S(1)}, s32[]{:T(128)}, ...), branch_computations={%region_9.15_spmd, %region_15.18_spmd} | conditional | flops 1258316928 | bytes 50129932 | solution.py:274
  59.7 4.4 reshape.1433
  74.3 4.8 divide_convert_fusion.1
  95.5 7.2 collective-permute-done.1
  102.8 30.1 %conditional.12 = (f32[4,128,200]{1,2,0:T(8,128)}) conditional(s32[]{:T(128)} %convert_element_type.954, (f32[4,128,200]{1,2,0:T(8,128)S(1)}, f32[1,200]{1,0:T(1,128)S(1)}, f32[1,200]{1,0:T(1,128)S(1)}, bf16[200,1920]{1,0:T(8,128)(2,1)S(1)}, bf16[64,266]{1,0:T(8,128)(2,1)S(1)}, /*index=5*/bf16[8,128]{1,0:T(8,128)(2,1)S(1)}, s32[]{:T(128)}, ...), branch_computations={%region_18.24_spmd, %region_24.27_spmd} | conditional | flops 1258316928 | bytes 50129932 | solution.py:274
  109.2 4.4 reshape.1438
  123.9 4.8 divide_convert_fusion.2
  134.2 6.6 collective-permute-done.2
  140.9 33.3 %conditional.13 = (f32[4,128,200]{1,2,0:T(8,128)}) conditional(s32[]{:T(128)} %convert_element_type.954, (f32[4,128,200]{1,2,0:T(8,128)S(1)}, f32[1,200]{1,0:T(1,128)S(1)}, f32[1,200]{1,0:T(1,128)S(1)}, bf16[200,1920]{1,0:T(8,128)(2,1)S(1)}, bf16[64,266]{1,0:T(8,128)(2,1)S(1)}, /*index=5*/bf16[8,128]{1,0:T(8,128)(2,1)S(1)}, s32[]{:T(128)}, ...), branch_computations={%region_27.33_spmd, %region_33.36_spmd} | conditional | flops 1258316928 | bytes 50129932 | solution.py:274
  147.4 4.4 reshape.1443
  161.8 5.7 divide_convert_fusion.3
  176.3 5.1 collective-permute-done.3
  184.3 66.8 %conditional.15 = (f32[200]{0:T(256)S(1)}, f32[200]{0:T(256)S(1)}, f32[512000]{0:T(1024)}, f32[800]{0:T(1024)S(1)}, f32[200]{0:T(256)S(1)}, /*index=5*/f32[4,128,200]{1,2,0:T(8,128)}) conditional(s32[]{:T(128)} %convert_element_type.954, (f32[4,128,200]{1,2,0:T(8,128)S(1)}, f32[1,200]{1,0:T(1,128)S(1)}, f32[1,200]{1,0:T(1,128)S(1)}, ...), branch_computations={%region_45.59_spmd, %region_59.68_spmd} | conditional | flops 3259688960 | bytes 187215760 | solution.py:303
  195.1 4.6 reshape.1453
  202.3 4.2 multiply_convert_fusion.10
  222.2 5.8 convert_reduce_fusion.6
  230.7 5.2 convert_reduce_fusion.5
  252.5 7.6 collective-permute-done.4
  261.2 64.2 %conditional.16 = (f32[200]{0:T(256)S(1)}, f32[200]{0:T(256)S(1)}, f32[512000]{0:T(1024)}, f32[800]{0:T(1024)S(1)}, f32[200]{0:T(256)S(1)}, /*index=5*/f32[4,128,200]{1,2,0:T(8,128)}) conditional(s32[]{:T(128)} %convert_element_type.954, (f32[4,128,200]{1,2,0:T(8,128)S(1)}, f32[1,200]{1,0:T(1,128)S(1)}, f32[1,200]{1,0:T(1,128)S(1)}, ...), branch_computations={%region_68.82_spmd, %region_82.91_spmd} | conditional | flops 3259688960 | bytes 185577328 | solution.py:303
  271.4 4.4 reshape.1462
  298.4 5.8 convert_reduce_fusion.12
  306.9 5.2 convert_reduce_fusion.11
  326.8 7.6 collective-permute-done.5
  335.5 64.3 %conditional.17 = (f32[200]{0:T(256)S(1)}, f32[200]{0:T(256)S(1)}, f32[512000]{0:T(1024)}, f32[800]{0:T(1024)S(1)}, f32[200]{0:T(256)S(1)}, /*index=5*/f32[4,128,200]{1,2,0:T(8,128)}) conditional(s32[]{:T(128)} %convert_element_type.954, (f32[4,128,200]{1,2,0:T(8,128)S(1)}, f32[1,200]{1,0:T(1,128)S(1)}, f32[1,200]{1,0:T(1,128)S(1)}, ...), branch_computations={%region_91.105_spmd, %region_105.114_spmd} | conditional | flops 3259688960 | bytes 185577328 | solution.py:303
  345.7 4.4 reshape.1471
  372.7 5.8 convert_reduce_fusion.18
  381.2 5.2 convert_reduce_fusion.17
  401.2 7.6 collective-permute-done.6
  409.9 64.2 %conditional.18 = (f32[200]{0:T(256)S(1)}, f32[200]{0:T(256)S(1)}, f32[512000]{0:T(1024)}, f32[800]{0:T(1024)S(1)}, f32[200]{0:T(256)S(1)}, /*index=5*/f32[4,128,200]{1,2,0:T(8,128)}) conditional(s32[]{:T(128)} %convert_element_type.954, (f32[4,128,200]{1,2,0:T(8,128)S(1)}, f32[1,200]{1,0:T(1,128)S(1)}, f32[1,200]{1,0:T(1,128)S(1)}, ...), branch_computations={%region_114.128_spmd, %region_128.137_spmd} | conditional | flops 3259688960 | bytes 185577328 | solution.py:303
  420.1 4.4 reshape.1480
  447.1 5.8 convert_reduce_fusion.24
  455.6 5.2 convert_reduce_fusion.23
  478.4 5.2 collective-permute-done.7
  484.6 61.3 %conditional.19 = (f32[200]{0:T(256)S(1)}, f32[200]{0:T(256)S(1)}, f32[512000]{0:T(1024)}, f32[800]{0:T(1024)S(1)}, f32[200]{0:T(256)S(1)}, /*index=5*/f32[4,128,200]{1,2,0:T(8,128)S(1)}) conditional(s32[]{:T(128)} %convert_element_type.954, (f32[4,128,200]{1,2,0:T(8,128)S(1)}, f32[1,200]{1,0:T(1,128)S(1)}, f32[1,200]{1,0:T(1,128)S(1)}, ...), branch_computations={%region_137.151_spmd, %region_151.160_spmd} | conditional | flops 3259688960 | bytes 182949392 | solution.py:303
  494.0 4.4 reshape.1489
  520.3 5.8 convert_reduce_fusion.30
  528.8 5.2 convert_reduce_fusion.29
  549.0 4.5 broadcast_multiply_fusion.70
  557.0 27.6 %conditional.14 = (f32[4,128,200]{1,2,0:T(8,128)S(1)}) conditional(s32[]{:T(128)} %convert_element_type.954, (f32[4,128,200]{1,2,0:T(8,128)S(1)}, f32[1,200]{1,0:T(1,128)S(1)}, f32[1,200]{1,0:T(1,128)S(1)}, bf16[200,1920]{1,0:T(8,128)(2,1)S(1)}, bf16[64,266]{1,0:T(8,128)(2,1)S(1)}, /*index=5*/bf16[8,128]{1,0:T(8,128)(2,1)S(1)}, s32[]{:T(128)}, ...), branch_computations={%region_36.42_spmd, %region_42.45_spmd} | conditional | flops 1258316928 | bytes 52751400 | solution.py:274
  563.6 4.4 reshape.1448
  578.5 4.6 divide_convert_fusion.4
  588.1 89.8 %all-reduce.5 = (f32[2,2,200]{2,1,0:T(2,128)}, f32[2,2,200]{2,1,0:T(2,128)}, f32[2,200]{1,0:T(2,128)}, f32[2,800]{1,0:T(2,128)}, f32[2,200]{1,0:T(2,128)}) all-reduce(f32[2,2,200]{2,1,0:T(2,128)S(1)} %get-tuple-element.1425, f32[2,2,200]{2,1,0:T(2,128)S(1)} %get-tuple-element.1424, ...), channel_id=1, replica_groups=mesh['dp'=32,'section'=4] {'dp','section'}, use_global_device_ids=true, to_apply=%region_160.161 | all-reduce | flops 4000 | bytes 32000 | tf_op jit(solution)/shard_map/psum | solution.py:330
  678.0 60.2 %all-reduce.9.cloned.1.call-done = (f32[2,512000]{1,0:T(2,128)}, f32[2,512000]{1,0:T(2,128)}) async-done(((f32[2,512000]{1,0:T(2,128)}, f32[2,512000]{1,0:T(2,128)}), (f32[2,512000]{1,0:T(2,128)}, f32[2,512000]{1,0:T(2,128)})) %all-reduce.9.cloned.1.call-update) | async-done | bytes 8192016 | tf_op jit(solution)/shard_map/psum | solution.py:330
  745.1 5.2 reshape.1504
  (675 shorter events, 396.8 us)
Async XLA Ops:
  7.2 5.8 copy-start
  7.2 731.0 %all-reduce.9.cloned.1.call-start = ((), (), s32[]{:S(2)}) async-start(), calls=%async_computation | async-start | bytes 16384000 | tf_op jit(solution)/shard_map/psum | solution.py:330
  13.2 127.7 %copy-start.153 = (f32[1,200]{1,0:T(1,128)}, f32[1,200]{1,0:T(1,128)S(1)}, u32[]{:S(2)}) copy-start(f32[1,200]{1,0:T(1,128)S(1)} %get-tuple-element.1430) | copy-start | bytes 2404
  13.2 127.7 %copy-start.155 = (f32[1,200]{1,0:T(1,128)}, f32[1,200]{1,0:T(1,128)S(1)}, u32[]{:S(2)}) copy-start(f32[1,200]{1,0:T(1,128)S(1)} %get-tuple-element.1431) | copy-start | bytes 2404
  14.3 38.8 %copy-start.63 = (bf16[8,128,200]{1,2,0:T(8,128)(2,1)S(1)}, bf16[8,128,200]{1,2,0:T(8,128)(2,1)}, u32[]{:S(2)}) copy-start(bf16[8,128,200]{1,2,0:T(8,128)(2,1)} %param.34) | copy-start | bytes 1228804
  43.5 9.8 %copy-start.74 = (f32[4,128,200]{1,2,0:T(8,128)}, f32[4,128,200]{1,2,0:T(8,128)S(1)}, u32[]{:S(2)}) copy-start(f32[4,128,200]{1,2,0:T(8,128)S(1)} %get-tuple-element.1097) | copy-start | bytes 1228804
  43.5 8.9 %collective-permute-start = (f32[4,128,200]{1,2,0:T(8,128)S(1)}, f32[4,128,200]{1,2,0:T(8,128)S(1)}, u32[]{:S(2)}, u32[]{:S(2)}) collective-permute-start(f32[4,128,200]{1,2,0:T(8,128)S(1)} %get-tuple-element.1097), channel_id=1, source_target_pairs={{0,1},{1,2},{2,3},{4,5},{5,6},{6,7},{8,9},{9,10},{10,11},{12,13},{... | collective-permute-start | bytes 1228808 | tf_op jit(solution)/shard_map/ppermute | solution.py:22
  94.1 8.6 %collective-permute-start.1 = (f32[4,128,200]{1,2,0:T(8,128)}, f32[4,128,200]{1,2,0:T(8,128)S(1)}, u32[]{:S(2)}, u32[]{:S(2)}) collective-permute-start(f32[4,128,200]{1,2,0:T(8,128)} %get-tuple-element.1098), channel_id=1, source_target_pairs={{0,1},{1,2},{2,3},{4,5},{5,6},{6,7},{8,9},{9,10},{10,11},{12,13},{... | collective-permute-start | bytes 1228808 | tf_op jit(solution)/shard_map/ppermute | solution.py:22
  132.8 7.9 %collective-permute-start.2 = (f32[4,128,200]{1,2,0:T(8,128)}, f32[4,128,200]{1,2,0:T(8,128)S(1)}, u32[]{:S(2)}, u32[]{:S(2)}) collective-permute-start(f32[4,128,200]{1,2,0:T(8,128)} %get-tuple-element.1099), channel_id=1, source_target_pairs={{0,1},{1,2},{2,3},{4,5},{5,6},{6,7},{8,9},{9,10},{10,11},{12,13},{... | collective-permute-start | bytes 1228808 | tf_op jit(solution)/shard_map/ppermute | solution.py:22
  140.9 34.7 %copy-start.17 = (f32[8,128,200]{1,2,0:T(8,128)S(1)}, f32[8,128,200]{1,2,0:T(8,128)}, u32[]{:S(2)}) copy-start(f32[8,128,200]{1,2,0:T(8,128)} %param.37) | copy-start | bytes 2457604
  174.2 7.3 collective-permute-start.3
  201.9 13.4 %copy-start.38 = (bf16[4,128,1,10,64]{1,0,4,3,2:T(4,128)(2,1)}, bf16[4,128,1,10,64]{1,0,4,3,2:T(4,128)(2,1)S(1)}, u32[]{:S(2)}) copy-start(bf16[4,128,1,10,64]{1,0,4,3,2:T(4,128)(2,1)S(1)} %get-tuple-element.1307) | copy-start | bytes 1966084 | tf_op jit(solution)/shard_map/cond
  206.5 10.1 %copy-start.5 = (bf16[4,128,10,266]{1,3,2,0:T(8,128)(2,1)}, bf16[4,128,10,266]{1,3,2,0:T(8,128)(2,1)S(1)}, u32[]{:S(2)}) copy-start(bf16[4,128,10,266]{1,3,2,0:T(8,128)(2,1)S(1)} %get-tuple-element.1316) | copy-start | bytes 8171524 | tf_op jit(solution)/shard_map/cond
  230.7 5.3 copy-start.29
  251.2 10.0 %copy-start.111 = (f32[800]{0:T(1024)}, f32[800]{0:T(1024)S(1)}, u32[]{:S(2)}) copy-start(f32[800]{0:T(1024)S(1)} %get-tuple-element.761) | copy-start | bytes 9604
  251.2 10.0 %copy-start.118 = (f32[200]{0:T(256)}, f32[200]{0:T(256)S(1)}, u32[]{:S(2)}) copy-start(f32[200]{0:T(256)S(1)} %get-tuple-element.756) | copy-start | bytes 2404
  251.2 10.0 %copy-start.129 = (f32[200]{0:T(256)}, f32[200]{0:T(256)S(1)}, u32[]{:S(2)}) copy-start(f32[200]{0:T(256)S(1)} %get-tuple-element.741) | copy-start | bytes 2404
  251.2 10.0 %copy-start.131 = (f32[200]{0:T(256)}, f32[200]{0:T(256)S(1)}, u32[]{:S(2)}) copy-start(f32[200]{0:T(256)S(1)} %get-tuple-element.746) | copy-start | bytes 2404
  251.2 8.9 %collective-permute-start.4 = (f32[4,128,200]{1,2,0:T(8,128)}, f32[4,128,200]{1,2,0:T(8,128)S(1)}, u32[]{:S(2)}, u32[]{:S(2)}) collective-permute-start(f32[4,128,200]{1,2,0:T(8,128)} %get-tuple-element.1102), channel_id=1, source_target_pairs={{1,0},{2,1},{3,2},{5,4},{6,5},{7,6},{9,8},{10,9},{11,10},{13,12},{... | collective-permute-start | bytes 1228808 | tf_op jit(solution)/shard_map/ppermute | solution.py:22
  278.0 13.4 %copy-start.40 = (bf16[4,128,1,10,64]{1,0,4,3,2:T(4,128)(2,1)}, bf16[4,128,1,10,64]{1,0,4,3,2:T(4,128)(2,1)S(1)}, u32[]{:S(2)}) copy-start(bf16[4,128,1,10,64]{1,0,4,3,2:T(4,128)(2,1)S(1)} %get-tuple-element.1327) | copy-start | bytes 1966084 | tf_op jit(solution)/shard_map/cond
  282.6 10.1 %copy-start.7 = (bf16[4,128,10,266]{1,3,2,0:T(8,128)(2,1)}, bf16[4,128,10,266]{1,3,2,0:T(8,128)(2,1)S(1)}, u32[]{:S(2)}) copy-start(bf16[4,128,10,266]{1,3,2,0:T(8,128)(2,1)S(1)} %get-tuple-element.1336) | copy-start | bytes 8171524 | tf_op jit(solution)/shard_map/cond
  306.9 5.3 copy-start.31
  325.5 10.0 %copy-start.113 = (f32[800]{0:T(1024)}, f32[800]{0:T(1024)S(1)}, u32[]{:S(2)}) copy-start(f32[800]{0:T(1024)S(1)} %get-tuple-element.762) | copy-start | bytes 9604
  325.5 10.0 %copy-start.120 = (f32[200]{0:T(256)}, f32[200]{0:T(256)S(1)}, u32[]{:S(2)}) copy-start(f32[200]{0:T(256)S(1)} %get-tuple-element.757) | copy-start | bytes 2404
  325.5 10.0 %copy-start.133 = (f32[200]{0:T(256)}, f32[200]{0:T(256)S(1)}, u32[]{:S(2)}) copy-start(f32[200]{0:T(256)S(1)} %get-tuple-element.742) | copy-start | bytes 2404
  325.5 10.0 %copy-start.135 = (f32[200]{0:T(256)}, f32[200]{0:T(256)S(1)}, u32[]{:S(2)}) copy-start(f32[200]{0:T(256)S(1)} %get-tuple-element.747) | copy-start | bytes 2404
  325.5 8.9 %collective-permute-start.5 = (f32[4,128,200]{1,2,0:T(8,128)}, f32[4,128,200]{1,2,0:T(8,128)S(1)}, u32[]{:S(2)}, u32[]{:S(2)}) collective-permute-start(f32[4,128,200]{1,2,0:T(8,128)} %get-tuple-element.1103), channel_id=1, source_target_pairs={{1,0},{2,1},{3,2},{5,4},{6,5},{7,6},{9,8},{10,9},{11,10},{13,12},{... | collective-permute-start | bytes 1228808 | tf_op jit(solution)/shard_map/ppermute | solution.py:22
  335.4 74.4 %copy-start.3 = (f32[4,128,200]{1,2,0:T(8,128)S(1)}, f32[4,128,200]{1,2,0:T(8,128)}, u32[]{:S(2)}) copy-start(f32[4,128,200]{1,2,0:T(8,128)} %get-tuple-element.1412) | copy-start | bytes 1228804
  352.3 13.4 %copy-start.42 = (bf16[4,128,1,10,64]{1,0,4,3,2:T(4,128)(2,1)}, bf16[4,128,1,10,64]{1,0,4,3,2:T(4,128)(2,1)S(1)}, u32[]{:S(2)}) copy-start(bf16[4,128,1,10,64]{1,0,4,3,2:T(4,128)(2,1)S(1)} %get-tuple-element.1347) | copy-start | bytes 1966084 | tf_op jit(solution)/shard_map/cond
  356.9 10.1 %copy-start.9 = (bf16[4,128,10,266]{1,3,2,0:T(8,128)(2,1)}, bf16[4,128,10,266]{1,3,2,0:T(8,128)(2,1)S(1)}, u32[]{:S(2)}) copy-start(bf16[4,128,10,266]{1,3,2,0:T(8,128)(2,1)S(1)} %get-tuple-element.1356) | copy-start | bytes 8171524 | tf_op jit(solution)/shard_map/cond
  381.2 5.3 copy-start.33
  399.9 10.0 %copy-start.115 = (f32[800]{0:T(1024)}, f32[800]{0:T(1024)S(1)}, u32[]{:S(2)}) copy-start(f32[800]{0:T(1024)S(1)} %get-tuple-element.763) | copy-start | bytes 9604
  399.9 10.0 %copy-start.122 = (f32[200]{0:T(256)}, f32[200]{0:T(256)S(1)}, u32[]{:S(2)}) copy-start(f32[200]{0:T(256)S(1)} %get-tuple-element.758) | copy-start | bytes 2404
  399.9 10.0 %copy-start.137 = (f32[200]{0:T(256)}, f32[200]{0:T(256)S(1)}, u32[]{:S(2)}) copy-start(f32[200]{0:T(256)S(1)} %get-tuple-element.743) | copy-start | bytes 2404
  399.9 10.0 %copy-start.139 = (f32[200]{0:T(256)}, f32[200]{0:T(256)S(1)}, u32[]{:S(2)}) copy-start(f32[200]{0:T(256)S(1)} %get-tuple-element.748) | copy-start | bytes 2404
  399.9 8.9 %collective-permute-start.6 = (f32[4,128,200]{1,2,0:T(8,128)}, f32[4,128,200]{1,2,0:T(8,128)S(1)}, u32[]{:S(2)}, u32[]{:S(2)}) collective-permute-start(f32[4,128,200]{1,2,0:T(8,128)} %get-tuple-element.1104), channel_id=1, source_target_pairs={{1,0},{2,1},{3,2},{5,4},{6,5},{7,6},{9,8},{10,9},{11,10},{13,12},{... | collective-permute-start | bytes 1228808 | tf_op jit(solution)/shard_map/ppermute | solution.py:22
  409.9 74.8 %copy-start.2 = (f32[4,128,200]{1,2,0:T(8,128)S(1)}, f32[4,128,200]{1,2,0:T(8,128)}, u32[]{:S(2)}) copy-start(f32[4,128,200]{1,2,0:T(8,128)} %get-tuple-element.1411) | copy-start | bytes 1228804
  426.7 13.4 %copy-start.44 = (bf16[4,128,1,10,64]{1,0,4,3,2:T(4,128)(2,1)}, bf16[4,128,1,10,64]{1,0,4,3,2:T(4,128)(2,1)S(1)}, u32[]{:S(2)}) copy-start(bf16[4,128,1,10,64]{1,0,4,3,2:T(4,128)(2,1)S(1)} %get-tuple-element.1367) | copy-start | bytes 1966084 | tf_op jit(solution)/shard_map/cond
  431.3 10.1 %copy-start.11 = (bf16[4,128,10,266]{1,3,2,0:T(8,128)(2,1)}, bf16[4,128,10,266]{1,3,2,0:T(8,128)(2,1)S(1)}, u32[]{:S(2)}) copy-start(bf16[4,128,10,266]{1,3,2,0:T(8,128)(2,1)S(1)} %get-tuple-element.1376) | copy-start | bytes 8171524 | tf_op jit(solution)/shard_map/cond
  455.6 5.3 copy-start.35
  474.2 10.5 %copy-start.124 = (f32[200]{0:T(256)}, f32[200]{0:T(256)S(1)}, u32[]{:S(2)}) copy-start(f32[200]{0:T(256)S(1)} %get-tuple-element.759) | copy-start | bytes 2404
  474.7 8.9 %collective-permute-start.7 = (f32[4,128,200]{1,2,0:T(8,128)}, f32[4,128,200]{1,2,0:T(8,128)S(1)}, u32[]{:S(2)}, u32[]{:S(2)}) collective-permute-start(f32[4,128,200]{1,2,0:T(8,128)} %get-tuple-element.1105), channel_id=1, source_target_pairs={{1,0},{2,1},{3,2},{5,4},{6,5},{7,6},{9,8},{10,9},{11,10},{13,12},{... | collective-permute-start | bytes 1228808 | tf_op jit(solution)/shard_map/ppermute | solution.py:22
  500.5 12.8 %copy-start.46 = (bf16[4,128,1,10,64]{1,0,4,3,2:T(4,128)(2,1)}, bf16[4,128,1,10,64]{1,0,4,3,2:T(4,128)(2,1)S(1)}, u32[]{:S(2)}) copy-start(bf16[4,128,1,10,64]{1,0,4,3,2:T(4,128)(2,1)S(1)} %get-tuple-element.1387) | copy-start | bytes 1966084 | tf_op jit(solution)/shard_map/cond
  505.1 9.5 %copy-start.13 = (bf16[4,128,10,266]{1,3,2,0:T(8,128)(2,1)}, bf16[4,128,10,266]{1,3,2,0:T(8,128)(2,1)S(1)}, u32[]{:S(2)}) copy-start(bf16[4,128,10,266]{1,3,2,0:T(8,128)(2,1)S(1)} %get-tuple-element.1396) | copy-start | bytes 8171524 | tf_op jit(solution)/shard_map/cond
  528.8 5.3 copy-start.37
  586.4 91.5 %copy-start.77 = (f32[4,128,200]{1,2,0:T(8,128)S(1)}, f32[4,128,200]{1,2,0:T(8,128)}, u32[]{:S(2)}) copy-start(f32[4,128,200]{1,2,0:T(8,128)} %copy-done.76) | copy-start | bytes 1228804
  678.0 60.2 %copy-start.86 = (f32[1,8,128,200]{2,3,1,0:T(8,128)}, f32[1,8,128,200]{2,3,1,0:T(8,128)S(1)}, u32[]{:S(2)}) copy-start(f32[1,8,128,200]{2,3,1,0:T(8,128)S(1)} %bitcast_dynamic-update-slice_fusion) | copy-start | bytes 2457604
  758.6 5.3 copy-start.1
  (105 other events, 201.7 us)
Sparse Core Ops, SparseCore 0:
  553.6 184.5 all-reduce.8
where the time goes:
time: 784 us; the launch traced here: 771 us
  matrix products  252 us (32%)
  local copies, waits for them, and re-layouts  215 us (27%)
  waiting for transfers between devices  115 us (15%)
  blocking collectives  89.8 us (11%)
  other arithmetic  57 us (7%)
  loops' own time  16.6 us (2%)
  between operations  15.8 us (2%)
  starting transfers between devices  10.5 us (1%)
    psum x1, blocking collectives, body(): lax.psum((slot_hot[..., None] * gain_grad, slot_hot[..., None] * shift_gr...  89.8 us
    dot_general x20, matrix products, feature_logits(): jnp.einsum('cnhe,ef->cnhf', vectors, random_map, preferred_element_type=j...  66.5 us
    psum x1, waiting for transfers between devices, body(): lax.psum((slot_hot[..., None] * gain_grad, slot_hot[..., None] * shift_gr...  60.2 us
    ppermute x8, waiting for transfers between devices, from_behind(): return lax.ppermute(value, axis, pairs)  54.4 us
    reshape x10, local copies, waits for them, and re-layouts, attend_forward(): projected.reshape(cell_count, slot_count, 3, HEADS, inner_width // HEADS)  44 us
    convert_element_type x10, local copies, waits for them, and re-layouts, attend_forward(): jnp.dot(normed_low, qkv_mats, preferred_element_type=jnp.float32)  40.1 us
    dot_general x5, matrix products, attend_backward(): jnp.einsum('cnhe,chfe->cnhf', grad_num, key_value, preferred_element_type...  28.8 us
    dot_general x10, matrix products, attend_forward(): jnp.einsum('cnhf,chfe->cnhe', query_feat, key_value, preferred_element_ty...  28.8 us
  transfers between devices with their start and end apart: 9, of which 9 were waited for; matrix products, arithmetic and copies ran while one was open for 4% of the time, Pallas kernels for 0%

commit v1 on v0

v1 whole, which is shorter than its diff:
```python
import math

import jax
import jax.numpy as jnp
from jax import lax
from jax.experimental import pallas as pl
from jax.experimental.pallas import tpu as pltpu
from jax.sharding import PartitionSpec as P

D = 200
HEADS = 10
HEAD_DIM = 64
FEATS = 266
FF = 800
INNER = HEADS * HEAD_DIM
LAYERS = 2
SLOTS = 128
EPSILON = 1e-05

PAIRS = HEADS // 2
MAIN = 256
TAIL = FEATS - MAIN
PAIR_W = 2 * MAIN + 128

LOG2E = math.log2(math.e)
S_FEAT = HEAD_DIM ** (-0.25)
S_NORM = HEAD_DIM ** (-0.5)
Q_SCALE = S_FEAT * LOG2E
SQ_SCALE = 0.5 * S_NORM * LOG2E
SQ_SHIFT = 0.5 * math.log2(FEATS) / HEAD_DIM
MASK_SHIFT = 1000.0
TOTAL_BACK = S_NORM / Q_SCALE

COL = 200
EARLY = [("out", j) for j in range(5)] + [("up", j) for j in range(7)] + [("down", j) for j in range(7)]
D_ROW, E_ROW, C_ROW, A_ROW, B_ROW, G_ROWS = 0, 2048, 3072, 7168, 11264, 14336


def place_columns():
    rows = {}

    def put(l, columns, at):
        for column in columns:
            rows[(l,) + column] = at
            at += COL
        return at

    qkv = [("qkv", j) for j in range(15)]
    ends = [
        put(0, qkv[0:10], D_ROW) + 24,
        put(0, qkv[10:], E_ROW),
        put(0, EARLY, C_ROW),
        put(1, EARLY, A_ROW),
        put(1, qkv, B_ROW) + 24,
    ]
    return rows, ends


ROWS, ENDS = place_columns()
SMALL_ROW = (ENDS[0] - 24, ENDS[4] - 24)

BF = jnp.bfloat16
F32 = jnp.float32


def mm(a, b):
    return jnp.dot(a, b, preferred_element_type=F32)


def mm_t(a, b):
    return lax.dot_general(a, b, (((1,), (1,)), ((), ())), preferred_element_type=F32)


def norm_forward(rows):
    centered = rows - jnp.mean(rows, axis=-1, keepdims=True)
    inverse = lax.rsqrt(jnp.mean(centered * centered, axis=-1, keepdims=True) + EPSILON)
    return centered * inverse, inverse


def build_maps(feats_ref, fw):
    ones = jnp.full((HEAD_DIM, MAIN), -1.0, BF)
    row = lax.broadcasted_iota(jnp.int32, (FEATS, 128), 0)
    lane = lax.broadcasted_iota(jnp.int32, (FEATS, 128), 1)
    tail_lane = lax.broadcasted_iota(jnp.int32, (HEAD_DIM, 128), 1)
    for l in range(LAYERS):
        f = feats_ref[l]
        fw[l, :, 0 : 2 * MAIN] = jnp.zeros((256, 2 * MAIN), BF)
        for hh in range(2):
            pick = jnp.where(row - MAIN == lane - TAIL * hh, 1.0, 0.0)
            pick = jnp.where(row >= MAIN, pick, 0.0).astype(BF)
            tail = mm(f, pick).astype(BF)
            minus = jnp.where(
                (tail_lane >= TAIL * hh) & (tail_lane < TAIL * (hh + 1)), -1.0, 0.0
            ).astype(BF)
            r = HEAD_DIM * hh
            fw[l, r : r + HEAD_DIM, MAIN * hh : MAIN * (hh + 1)] = f[:, 0:MAIN]
            fw[l, 128 + r : 128 + r + HEAD_DIM, MAIN * hh : MAIN * (hh + 1)] = ones
            fw[l, r : r + HEAD_DIM, 2 * MAIN : PAIR_W] = tail
            fw[l, 128 + r : 128 + r + HEAD_DIM, 2 * MAIN : PAIR_W] = minus


def tail_mask():
    row = lax.broadcasted_iota(jnp.int32, (256, 128), 0)
    lane = lax.broadcasted_iota(jnp.int32, (256, 128), 1)
    odd = (row % 128) >= HEAD_DIM
    low = jnp.where(odd, TAIL, 0)
    return jnp.where((lane >= low) & (lane < low + TAIL), 1.0, 0.0)


def store_blocks(target, left, right, mask):
    for hh in range(2):
        r = HEAD_DIM * hh
        lhs = jnp.concatenate(
            [left[r : r + HEAD_DIM], left[128 + r : 128 + r + HEAD_DIM]], axis=0
        )
        block = mm(lhs, right[:, MAIN * hh : MAIN * (hh + 1)]).astype(BF)
        target[r : r + HEAD_DIM, MAIN * hh : MAIN * (hh + 1)] = block[0:HEAD_DIM]
        target[128 + r : 128 + r + HEAD_DIM, MAIN * hh : MAIN * (hh + 1)] = block[HEAD_DIM:]
    target[:, 2 * MAIN : PAIR_W] = (mm(left, right[:, 2 * MAIN : PAIR_W]) * mask).astype(BF)


def pack_columns(g, l, kind, value, columns=None):
    width = value.shape[1]
    columns = range(pl.cdiv(width, 128)) if columns is None else columns
    for n, j in enumerate(columns):
        take = min(128, width - 128 * n)
        at = ROWS[l, kind, j]
        g[at : at + COL, 0:take] = value[:, 128 * n : 128 * n + take]


def pack_row(g, l, row, value):
    width = value.shape[1]
    for j in range(pl.cdiv(width, 128)):
        take = min(128, width - 128 * j)
        at = SMALL_ROW[l] + row + j
        g[at : at + 1, 0:take] = value[:, 128 * j : 128 * j + take]


def clear_gaps(g):
    def clear(start, end):
        if end > start:
            g[start:end, :] = jnp.zeros((end - start, 128), F32)

    for end, limit in zip(ENDS, (E_ROW, C_ROW, A_ROW, B_ROW, G_ROWS)):
        clear(end, limit)
    for l in range(LAYERS):
        clear(SMALL_ROW[l], SMALL_ROW[l] + 24)
        for kind in ("up", "down"):
            clear(ROWS[l, kind, 6], ROWS[l, kind, 6] + COL)


def layers_kernel(
    inputs_hbm,
    lengths,
    gene_mask,
    out_grad_hbm,
    gain,
    bias,
    wqkv_hbm,
    wout_hbm,
    bout,
    feats,
    wup_hbm,
    bup,
    wdown_hbm,
    bdown,
    acts_out,
    sg_out,
    out,
    wqkv,
    wout,
    wup,
    wdown,
    x_in,
    x,
    gr,
    xhat,
    inv,
    normed,
    fw,
    zc,
    vs,
    vt,
    phi,
    kv,
    rden,
    att,
    dn,
    dn_t,
    dqkv,
    hid,
    gp,
    acts,
    sgrads,
    kept,
    g,
    own,
    hop1,
    near1,
    t1,
    near2,
    last,
    relay,
    sems,
    send_sems,
    recv_sems,
    local_sems,
):
    place = Place()
    wire = Wire(send_sems, recv_sems)
    greet(place)
    parts, before = {}, 0
    for name, t, axes, kind in PARTS:
        bufs = (own, hop1, near1, t1, near2, last)
        parts[name] = Part(place, wire, t, axes, kind, before, g, out, bufs)
        before += t
    act_stream = Streams(place, wire, acts, acts_out, relay.at[0])
    sg_stream = Streams(place, wire, sgrads, sg_out, relay.at[1])

    def advance(names):
        for name in names.split():
            if name == "acts":
                act_stream.forward()
            else:
                parts[name].advance()

    section = lax.axis_index("section")
    first = section * 2
    copy_in = pltpu.make_async_copy(inputs_hbm.at[pl.ds(first, 2)], x_in, sems.at[0])
    copy_gr = pltpu.make_async_copy(out_grad_hbm.at[pl.ds(first, 2)], gr, sems.at[1])
    copy_in.start()
    loads = {}
    for l in range(LAYERS):
        for n, (name, src, dst) in enumerate(
            (
                ("qkv", wqkv_hbm, wqkv),
                ("out", wout_hbm, wout),
                ("up", wup_hbm, wup),
                ("down", wdown_hbm, wdown),
            )
        ):
            loads[name, l] = pltpu.make_async_copy(src.at[l], dst.at[l], sems.at[2 + 4 * l + n])
            loads[name, l].start()
    copy_gr.start()
    build_maps(feats, fw)
    mask = tail_mask()
    ones_rows = jnp.ones((128, 128), BF)

    blank = jnp.zeros((LAYERS, 2, PAIRS, HEAD_DIM, MAIN), BF)
    for r in range(4):
        side = MAIN * (1 - r % 2)
        kv[:, :, :, HEAD_DIM * r : HEAD_DIM * (r + 1), side : side + MAIN] = blank
    clear_gaps(g)

    slot = lax.broadcasted_iota(jnp.int32, (128, 128), 1)
    shift = []
    for c in range(2):
        marks = jnp.broadcast_to(gene_mask[pl.ds(first + c, 1), :], (128, 128))
        live = (slot < lengths[first + c]) & (marks > 0)
        shift.append(jnp.where(live, SQ_SHIFT, MASK_SHIFT).T)
    key_shift = jnp.concatenate(shift, axis=0)

    copy_in.wait()
    x[...] = jnp.concatenate([x_in[0].T, x_in[1].T], axis=0).astype(F32)

    def attend_forward(l):
        nx, iv = norm_forward(x[...])
        xhat[l, 0] = nx
        inv[l, 0] = iv
        nb = (nx * gain[l, 0:1] + bias[l, 0:1]).astype(BF)
        normed[l, 0] = nb
        loads["qkv", l].wait()
        for side, shift in ((0, SQ_SHIFT), (1, key_shift)):
            value = mm(nb, wqkv[l, :, INNER * side : INNER * (side + 1)])
            for p in range(PAIRS):
                part = value[:, 128 * p : 128 * (p + 1)]
                zc[l, side, p, :, 0:128] = (part * Q_SCALE).astype(BF)
                zc[l, side, p, :, 128:256] = (part * part * SQ_SCALE + shift).astype(BF)
        v = mm(nb, wqkv[l, :, 2 * INNER : 3 * INNER]).astype(BF)
        vs[l] = v
        vt[...] = v.T

        for side in range(2):
            z = mm(zc[l, side].reshape(PAIRS * 256, 256), fw[l])
            phi[l, side] = jnp.exp2(z).astype(BF).reshape(PAIRS, 256, PAIR_W)
        for p in range(PAIRS):
            for c in range(2):
                rows = slice(128 * c, 128 * (c + 1))
                left = jnp.concatenate([vt[128 * p : 128 * (p + 1), rows], ones_rows], axis=0)
                store_blocks(kv.at[l, c, p], left, phi[l, 1, p, rows], mask)
        for p in range(PAIRS):
            lanes = slice(128 * p, 128 * (p + 1))
            for c in range(2):
                rows = slice(128 * c, 128 * (c + 1))
                nd = mm_t(phi[l, 0, p, rows], kv[l, c, p])
                rd = 1.0 / nd[:, 128:]
                rden[l, rows, lanes] = rd
                att[l, rows, lanes] = (nd[:, 0:128] * rd).astype(BF)
        loads["out", l].wait()
        x[...] = x[...] + mm_t(att[l], wout[l]) + bout[l : l + 1]

    def mix_forward(l):
        nx, iv = norm_forward(x[...])
        xhat[l, 1] = nx
        inv[l, 1] = iv
        nb = (nx * gain[l, 1:2] + bias[l, 1:2]).astype(BF)
        normed[l, 1] = nb
        loads["up", l].wait()
        loads["down", l].wait()
        pre = mm(nb, wup[l]) + bup[l : l + 1]
        cdf = 0.5 * (1.0 + lax.erf(pre * math.sqrt(0.5)))
        hid[l] = (pre * cdf).astype(BF)
        density = jnp.exp(-0.5 * pre * pre) * (1.0 / math.sqrt(2.0 * math.pi))
        gp[l] = (cdf + pre * density).astype(BF)
        x[...] = x[...] + mm_t(hid[l], wdown[l]) + bdown[l : l + 1]

    def norm_backward(l, j, grad_normed):
        nx = xhat[l, j]
        pack_row(g, l, 7 + 2 * j, jnp.sum(grad_normed * nx, axis=0, keepdims=True))
        pack_row(g, l, 11 + 2 * j, jnp.sum(grad_normed, axis=0, keepdims=True))
        scaled = grad_normed * gain[l, j : j + 1]
        return inv[l, j] * (
            scaled
            - jnp.mean(scaled, axis=-1, keepdims=True)
            - nx * jnp.mean(scaled * nx, axis=-1, keepdims=True)
        )

    def mix_backward(l, between):
        low = gr2[...].astype(BF)
        low_t = low.T
        pack_row(g, l, 17, jnp.sum(low.astype(F32), axis=0, keepdims=True))
        pack_columns(g, l, "down", mm(low_t, hid[l]))
        between("mix0")
        dpre = (mm(low, wdown[l]) * gp[l].astype(F32)).astype(BF)
        pack_row(g, l, 0, jnp.sum(dpre.astype(F32), axis=0, keepdims=True))
        between("mix1")
        pack_columns(g, l, "up", mm(normed[l, 1].T, dpre))
        between("mix2")
        gr2[...] = gr2[...] + norm_backward(l, 1, mm_t(dpre, wup[l]))
        between("mix3")

    def attend_backward(l, between):
        low = gr2[...].astype(BF)
        low_t = low.T
        pack_row(g, l, 15, jnp.sum(low.astype(F32), axis=0, keepdims=True))
        pack_columns(g, l, "out", mm(low_t, att[l]))
        datt = mm(low, wout[l])
        dnum = datt * rden[l]
        dden = -dnum * att[l].astype(F32)
        for p in range(PAIRS):
            lanes = slice(128 * p, 128 * (p + 1))
            dn[p, :, 0:128] = dnum[:, lanes].astype(BF)
            dn[p, :, 128:256] = dden[:, lanes].astype(BF)
            dn_t[p] = dn[p].T
        normed_t = normed[l, 0].T
        between("pre")
        for p in range(PAIRS):
            for c in range(2):
                rows = slice(128 * c, 128 * (c + 1))
                phi_q = phi[l, 0, p, rows]
                dzq = mm(dn[p, rows], kv[l, c, p]).astype(BF) * phi_q
                store_blocks(kv.at[l, c, p], dn_t[p, :, rows], phi_q, mask)
                phi[l, 0, p, rows] = dzq
            between(f"q{p}")
        for p in range(PAIRS):
            lanes = slice(128 * p, 128 * (p + 1))
            for c in range(2):
                rows = slice(128 * c, 128 * (c + 1))
                phi_k = phi[l, 1, p, rows]
                vh = jnp.concatenate([vs[l, rows, lanes], ones_rows], axis=1)
                dzk = mm(vh, kv[l, c, p]).astype(BF) * phi_k
                dv = mm_t(phi_k, kv[l, c, p, 0:128])
                dqkv[rows, 2 * INNER + 128 * p : 2 * INNER + 128 * (p + 1)] = dv.astype(BF)
                phi[l, 1, p, rows] = dzk
            if p == PAIRS - 1:
                pack_columns(g, l, "qkv", mm(normed_t, dqkv[:, 2 * INNER :]), range(10, 15))
            between(f"k{p}")

        for side in range(2):
            b = mm_t(phi[l, side].reshape(PAIRS * 256, PAIR_W), fw[l]).reshape(PAIRS, 256, 256)
            for p in range(PAIRS):
                own = zc[l, side, p, :, 0:128].astype(F32) * TOTAL_BACK
                value = b[p, :, 0:128] * S_FEAT + b[p, :, 128:256] * own
                at = INNER * side + 128 * p
                dqkv[:, at : at + 128] = value.astype(BF)
        between("back")
        pack_columns(g, l, "qkv", mm(normed_t, dqkv[:, 0 : 2 * INNER]), range(10))
        gr2[...] = gr2[...] + norm_backward(l, 0, mm_t(dqkv[...], wqkv[l]))
        between("post")

    gr2 = x

    def turn_stream(target, s, value):
        for c in range(2):
            target[s, c] = value[SLOTS * c : SLOTS * (c + 1)].T

    for l in range(LAYERS):
        attend_forward(l)
        turn_stream(acts, 2 * l, x[...])
        mix_forward(l)
        turn_stream(acts, 2 * l + 1, x[...])
    copy_gr.wait()
    gr2[...] = jnp.concatenate([gr[0].T, gr[1].T], axis=0)
    await_greetings(10)
    act_stream.start(local_sems.at[0])
    for l in reversed(range(LAYERS)):
        mix_backward(l, lambda at: advance(DURING[l].get(at, "")))
        kept[2 * l + 1] = gr2[...]
        attend_backward(l, lambda at: advance(DURING[l].get(at, "")))
        kept[2 * l] = gr2[...]
    for n, name in enumerate(BEHIND):
        if name == "sg":
            sg_stream.forward()
        else:
            parts[name].advance()
        if n == 2:
            for turn in range(2 * LAYERS):
                turn_stream(sgrads, turn, kept[turn])
            sg_stream.start(local_sems.at[1])
            act_stream.finish()
        wire.drain(max(len(wire.sent) - 72, 0))
    sg_stream.finish()
    wire.drain(len(wire.sent))


def layers(args):
    vmem = pl.BlockSpec(memory_space=pltpu.VMEM)
    hbm = pl.BlockSpec(memory_space=pl.ANY)
    smem = pl.BlockSpec(memory_space=pltpu.SMEM)
    rows = 2 * SLOTS

    def shape(*dims):
        return jax.ShapeDtypeStruct(dims, F32)

    def share(n, *lead):
        return pltpu.VMEM(lead + (n * SHARE, 128), F32)

    scratch = [
        pltpu.VMEM((LAYERS, D, 3 * INNER), BF),
        pltpu.VMEM((LAYERS, D, INNER), BF),
        pltpu.VMEM((LAYERS, D, FF), BF),
        pltpu.VMEM((LAYERS, D, FF), BF),
        pltpu.VMEM((2, D, SLOTS), BF),
        pltpu.VMEM((rows, D), F32),
        pltpu.VMEM((2, D, SLOTS), F32),
        pltpu.VMEM((LAYERS, 2, rows, D), F32),
        pltpu.VMEM((LAYERS, 2, rows, 1), F32),
        pltpu.VMEM((LAYERS, 2, rows, D), BF),
        pltpu.VMEM((LAYERS, 256, PAIR_W), BF),
        pltpu.VMEM((LAYERS, 2, PAIRS, rows, 256), BF),
        pltpu.VMEM((LAYERS, rows, INNER), BF),
        pltpu.VMEM((INNER, rows), BF),
        pltpu.VMEM((LAYERS, 2, PAIRS, rows, PAIR_W), BF),
        pltpu.VMEM((LAYERS, 2, PAIRS, 256, PAIR_W), BF),
        pltpu.VMEM((LAYERS, rows, INNER), F32),
        pltpu.VMEM((LAYERS, rows, INNER), BF),
        pltpu.VMEM((PAIRS, rows, 256), BF),
        pltpu.VMEM((PAIRS, 256, rows), BF),
        pltpu.VMEM((rows, 3 * INNER), BF),
        pltpu.VMEM((LAYERS, rows, FF), BF),
        pltpu.VMEM((LAYERS, rows, FF), BF),
        pltpu.VMEM((2 * LAYERS, 2, D, SLOTS), F32),
        pltpu.VMEM((2 * LAYERS, 2, D, SLOTS), F32),
        pltpu.VMEM((2 * LAYERS, rows, D), F32),
        share(1024),
        share(512),
        share(128),
        share(128, 3),
        share(128),
        share(32, 3),
        share(32, 4),
        pltpu.VMEM((2, 2, D, SLOTS), F32),
        pltpu.SemaphoreType.DMA((2 + 4 * LAYERS,)),
        pltpu.SemaphoreType.DMA((SENDS,)),
        pltpu.SemaphoreType.DMA((SENDS,)),
        pltpu.SemaphoreType.DMA((2,)),
    ]
    return pl.pallas_call(
        layers_kernel,
        out_shape=(
            pltpu.VMEM((8, D, SLOTS), F32),
            pltpu.VMEM((8, D, SLOTS), F32),
            pltpu.VMEM((1024 * SHARE, 128), F32),
        ),
        in_specs=[hbm, smem, vmem, hbm, vmem, vmem, hbm, hbm, vmem, vmem, hbm, vmem, hbm, vmem],
        out_specs=(vmem, vmem, vmem),
        scratch_shapes=scratch,
        compiler_params=pltpu.CompilerParams(
            vmem_limit_bytes=53 * 1024 * 1024, collective_id=0, has_side_effects=True
        ),
        name="layers",
    )(*args)


MESH = pl.DeviceIdType.MESH

PARTS = (
    ("D0", 1, "yzx", False),
    ("D1", 1, "zxy", False),
    ("E0", 1, "yxz", True),
    ("C0", 3, "xyz", True),
    ("C1", 1, "zxy", True),
    ("A0", 4, "zyx", True),
    ("B0", 3, "yxz", True),
)
SHARE = sum(part[1] for part in PARTS)
SENDS = 20 * len(PARTS) + 12

DURING = (
    {"pre": "C0 B0 C1", "k0": "A0", "k4": "E0", "back": "C0 C1 B0", "post": "D1 E0 D0"},
    {"pre": "A0", "k0": "acts", "post": "B0 A0"},
)
BEHIND = (
    "A0", "C1", "D1", "C0", "D0", "B0", "E0", "A0",
    "C0", "B0", "C1", "D0", "E0", "sg", "D1", "C0",
    "A0", "C1", "E0", "D1", "B0", "D0", "A0", "C0",
    "C1", "E0", "D1", "B0", "D0", "A0", "C0", "C1",
    "E0", "D1", "B0", "D0", "C0", "E0", "A0", "C1",
    "B0", "C0", "A0", "D1", "C1", "D0", "B0", "E0",
    "C0", "D1", "C1", "D0", "E0",
)


class Place:
    def __init__(self):
        self.dp = lax.axis_index("dp")
        self.section = lax.axis_index("section")
        self.core = lax.rem(self.dp, 2)
        self.at = {
            "x": lax.rem(self.dp // 2, 4),
            "y": self.dp // 8,
            "z": self.section,
        }

        self.ahead, self.behind = 1 + 2 * self.core, 3 - 2 * self.core
        self.steps, self.peers = {}, {}

    def step(self, axis, by):
        key = axis, by if isinstance(by, int) else id(by)
        if key not in self.steps:
            self.steps[key] = lax.rem(self.at[axis] + by, 4)
        return self.steps[key]

    def peer(self, axis, by):
        key = axis, by if isinstance(by, int) else id(by)
        if key not in self.peers:
            self.peers[key] = self.find_peer(axis, by)
        return self.peers[key]

    def find_peer(self, axis, by):
        if axis == "core":
            return {"dp": self.dp + 1 - 2 * self.core, "section": self.section}
        to = self.step(axis, by)
        if axis == "z":
            return {"dp": self.dp, "section": to}
        stride = 2 if axis == "x" else 8
        return {"dp": self.dp + stride * (to - self.at[axis]), "section": self.section}


class Wire:
    def __init__(self, send_sems, recv_sems):
        self.send_sems, self.recv_sems = send_sems, recv_sems
        self.sent = []
        self.drained = 0

    def send(self, src, dst, to):
        n = len(self.sent)
        copy = pltpu.make_async_remote_copy(
            src_ref=src,
            dst_ref=dst,
            send_sem=self.send_sems.at[n],
            recv_sem=self.recv_sems.at[n],
            device_id=to,
            device_id_type=MESH,
        )
        copy.start()
        self.sent.append(copy)
        return copy

    def drain(self, end):
        for copy in self.sent[self.drained : end]:
            copy.wait_send()
        self.drained = end


def greet(place):
    barrier = pltpu.get_barrier_semaphore()
    peers = [place.peer("core", 1)]
    peers += [place.peer(axis, by) for axis in "xyz" for by in (1, 2, 3)]
    for peer in peers:
        pl.semaphore_signal(barrier, inc=1, device_id=peer, device_id_type=MESH)


def await_greetings(count):
    pl.semaphore_wait(pltpu.get_barrier_semaphore(), count)


class Streams:
    def __init__(self, place, wire, source, target, relay):
        self.place, self.wire, self.source, self.target, self.relay = (
            place,
            wire,
            source,
            target,
            relay,
        )

    def start(self, local_sem):
        p, w = self.place, self.wire
        me, right, left, far = (p.step("z", by) for by in (0, 1, 3, 2))
        self.hops = [
            w.send(self.source.at[far, 0], self.relay.at[0], p.peer("z", 1)),
            w.send(self.source.at[far, 1], self.relay.at[1], p.peer("z", 3)),
        ]
        own = self.target.at[pl.ds(2 * me, 2)]
        self.direct = [
            w.send(self.source.at[right], own, p.peer("z", 1)),
            w.send(self.source.at[left], own, p.peer("z", 3)),
        ]
        self.local = pltpu.make_async_copy(self.source.at[me], own, local_sem)
        self.local.start()

    def forward(self):
        p, w = self.place, self.wire
        self.hops[0].wait_recv()
        self.direct.append(
            w.send(self.relay.at[0], self.target.at[2 * p.step("z", 3)], p.peer("z", 1))
        )
        self.hops[1].wait_recv()
        self.direct.append(
            w.send(self.relay.at[1], self.target.at[2 * p.step("z", 1) + 1], p.peer("z", 3))
        )

    def finish(self):
        for copy in self.direct:
            copy.wait_recv()
        self.local.wait()


class Quarters:
    def __init__(self, place, wire, axis, quarter):
        self.place, self.wire, self.axis, self.quarter = place, wire, axis, quarter

    def rows(self, by, base=0):
        start = base + self.place.step(self.axis, by) * self.quarter
        return pl.ds(pl.multiple_of(start, 8), self.quarter)

    def begin(self, block, near):
        self.block, self.near, self.got = block, near, []

    def send(self, by):
        src, dst = self.block.at[self.rows(by)], self.near.at[by - 1]
        self.got.append(self.wire.send(src, dst, self.place.peer(self.axis, by)))

    def result(self, block):
        for copy in self.got:
            copy.wait_recv()
        return (block[self.rows(0), :] + self.near[0]) + (self.near[1] + self.near[2])

    def spread(self, out, base):
        view = out.at[self.rows(0, base)]
        self.back = [
            self.wire.send(view, view, self.place.peer(self.axis, by)) for by in (2, 1, 3)
        ]

    def arrivals(self):
        return zip(self.back, (2, 3, 1))

    def spread_end(self):
        for copy in self.back:
            copy.wait_recv()


class Ring:
    def __init__(self, place, wire, axis, quarter):
        self.place, self.wire, self.axis, self.quarter = place, wire, axis, quarter
        self.ahead, self.behind = place.ahead, place.behind
        self.to_ahead = place.peer(axis, self.ahead)
        self.to_behind = place.peer(axis, self.behind)

    def buffers(self, hop, near):
        self.hop, self.near = hop, near

    def rows(self, by, base=0):
        start = base + self.place.step(self.axis, by) * self.quarter
        return pl.ds(pl.multiple_of(start, 8), self.quarter)

    def send_far(self, block):
        self.far = self.wire.send(block.at[self.rows(2)], self.hop, self.to_ahead)

    def send_near(self, block):
        src = block.at[self.rows(self.behind)]
        self.got = [self.wire.send(src, self.near.at[1], self.to_behind)]

    def send_sum(self, block):
        self.far.wait_recv()
        self.hop[...] = self.hop[...] + block[self.rows(self.ahead), :]
        self.got.append(self.wire.send(self.hop, self.near.at[0], self.to_ahead))

    def result(self, block):
        for copy in self.got:
            copy.wait_recv()
        return block[self.rows(0), :] + self.near[0] + self.near[1]

    def spread(self, out, base):
        w = self.wire
        view = out.at[self.rows(0, base)]
        self.first = w.send(view, view, self.to_ahead)
        self.others = [w.send(view, view, self.to_behind)]

    def spread_on(self, out, base):
        self.first.wait_recv()
        view = out.at[self.rows(self.behind, base)]
        self.others.append(self.wire.send(view, view, self.to_ahead))

    def arrivals(self):
        return zip(self.others, (self.ahead, 2))


class Part:
    def __init__(self, place, wire, tiles, axes, ring, before, g, out, bufs):
        self.place, self.wire, self.axes, self.g, self.out = place, wire, axes, g, out
        t, b = tiles, before
        self.t, self.b = t, b
        base, core = 1024 * b, place.core
        self.mine = pl.multiple_of(base + core * (512 * t), 8)
        self.other = pl.multiple_of(base + (1 - core) * (512 * t), 8)
        self.at1 = self.mine + place.at[axes[0]] * (128 * t)
        self.at2 = self.at1 + place.at[axes[1]] * (32 * t)
        own, hop1, near1, t1, near2, last = bufs
        self.own_all = own
        self.own = own.at[self.spot(512)]
        self.near1 = near1.at[:, self.spot(128)]
        self.t1 = t1.at[self.spot(128)]
        self.near2 = near2.at[:, self.spot(32)]
        self.last = last.at[:, self.spot(32)]
        self.phase2 = Quarters(place, wire, axes[1], 32 * t)
        self.at = 0
        if ring:
            self.phase1 = Ring(place, wire, axes[0], 128 * t)
            self.phase1.buffers(hop1.at[self.spot(128)], self.near1)
            self.steps = [
                self.swap,
                self.join_ring,
                self.sums,
                self.second,
                self.third,
                self.total,
                self.back1,
                self.back1_on,
                self.give_rest,
                self.taken,
            ]
        else:
            self.phase1 = Quarters(place, wire, axes[0], 128 * t)
            self.steps = [
                self.swap,
                self.join,
                self.second,
                self.third,
                self.total,
                self.back1,
                self.give_rest,
                self.taken,
            ]

    def advance(self):
        self.steps[self.at]()
        self.at += 1

    def spot(self, rows):
        return pl.ds(rows * self.b, rows * self.t)

    def swap(self):
        src = self.g.at[pl.ds(self.other, 512 * self.t)]
        self.swapped = self.wire.send(src, self.own, self.place.peer("core", 1))

    def add_quarter(self, by):
        rows = 128 * self.t
        start = self.place.step(self.axes[0], by) * rows
        to = pl.ds(pl.multiple_of(512 * self.b + start, 8), rows)
        mine = pl.ds(pl.multiple_of(self.mine + start, 8), rows)
        self.own_all[to, :] = self.own_all[to, :] + self.g[mine, :]

    def join(self):
        self.swapped.wait_recv()
        self.phase1.begin(self.own, self.near1)
        for by in (2, 1, 3):
            self.add_quarter(by)
            self.phase1.send(by)
        self.add_quarter(0)

    def join_ring(self):
        self.swapped.wait_recv()
        self.add_quarter(2)
        self.phase1.send_far(self.own)
        self.add_quarter(self.place.behind)
        self.phase1.send_near(self.own)
        self.add_quarter(self.place.ahead)
        self.add_quarter(0)

    def sums(self):
        self.phase1.send_sum(self.own)

    def second(self):
        self.t1[...] = self.phase1.result(self.own)
        self.phase2.begin(self.t1, self.near2)
        for by in (2, 1, 3):
            self.phase2.send(by)

    def third(self):
        here = self.place.at[self.axes[2]]
        self.last[here] = self.phase2.result(self.t1)
        view = self.last.at[here]
        self.thirds = [
            self.wire.send(view, view, self.place.peer(self.axes[2], by)) for by in (2, 1, 3)
        ]

    def total(self):
        for copy in self.thirds:
            copy.wait_recv()
        z = self.last
        rows = pl.ds(pl.multiple_of(self.at2, 8), 32 * self.t)
        self.out[rows, :] = (z[0] + z[1]) + (z[2] + z[3])
        self.phase2.spread(self.out, self.at1)

    def back1(self):
        self.phase2.spread_end()
        self.phase1.spread(self.out, self.mine)
        self.given = []
        self.give(0)

    def back1_on(self):
        self.phase1.spread_on(self.out, self.mine)
        self.give(self.place.behind)

    def give(self, by):
        view = self.out.at[self.phase1.rows(by, self.mine)]
        self.given.append(self.wire.send(view, view, self.place.peer("core", 1)))

    def give_rest(self):
        for copy, by in self.phase1.arrivals():
            copy.wait_recv()
            self.give(by)

    def taken(self):
        for copy in self.given:
            copy.wait_recv()


def finish_kernel(
    acts,
    sgrads,
    out,
    acts_out,
    sg_out,
    gains,
    shifts,
    qkv_out,
    out_out,
    bout,
    up_out,
    bup,
    down_out,
    bdown,
    qkv,
    out_w,
    up,
    down,
    sems,
):
    copies = []

    def start(src, dst):
        copies.append(pltpu.make_async_copy(src, dst, sems.at[len(copies)]))
        copies[-1].start()

    start(acts, acts_out)
    start(sgrads, sg_out)
    for l in range(LAYERS):
        for kind, target, result, width in (
            ("qkv", qkv, qkv_out, 3 * INNER),
            ("out", out_w, out_out, INNER),
            ("up", up, up_out, FF),
            ("down", down, down_out, FF),
        ):
            for j in range(pl.cdiv(width, 128)):
                take = min(128, width - 128 * j)
                at = ROWS[l, kind, j]
                target[l, :, 128 * j : 128 * j + take] = out[at : at + COL, 0:take]
            start(target.at[l], result.at[l])
    write_small(out, gains, shifts, bout, bup, bdown)
    for copy in copies:
        copy.wait()


def finish(acts, sgrads, out):
    vmem = pl.BlockSpec(memory_space=pltpu.VMEM)
    hbm = pl.BlockSpec(memory_space=pl.ANY)

    def shape(*dims):
        return jax.ShapeDtypeStruct(dims, F32)

    return pl.pallas_call(
        finish_kernel,
        out_shape=(
            shape(8, D, SLOTS),
            shape(8, D, SLOTS),
            shape(LAYERS, 2, D),
            shape(LAYERS, 2, D),
            shape(LAYERS, D, 3 * INNER),
            shape(LAYERS, D, INNER),
            shape(LAYERS, D),
            shape(LAYERS, D, FF),
            shape(LAYERS, FF),
            shape(LAYERS, D, FF),
            shape(LAYERS, D),
        ),
        in_specs=[vmem, vmem, vmem],
        out_specs=(hbm, hbm, vmem, vmem, hbm, hbm, vmem, hbm, vmem, hbm, vmem),
        scratch_shapes=[
            pltpu.VMEM((LAYERS, D, 3 * INNER), F32),
            pltpu.VMEM((LAYERS, D, INNER), F32),
            pltpu.VMEM((LAYERS, D, FF), F32),
            pltpu.VMEM((LAYERS, D, FF), F32),
            pltpu.SemaphoreType.DMA((2 + 4 * LAYERS,)),
        ],
        compiler_params=pltpu.CompilerParams(vmem_limit_bytes=24 * 1024 * 1024),
        name="finish",
    )(acts, sgrads, out)


def write_small(out, gains, shifts, bout, bup, bdown):
    for l in range(LAYERS):

        def row(at, width):
            start = SMALL_ROW[l] + at
            rows = [out[start + j : start + j + 1, :] for j in range(pl.cdiv(width, 128))]
            return jnp.concatenate(rows, axis=1)[:, 0:width]

        for j in range(2):
            gains[l, j : j + 1, :] = row(7 + 2 * j, D)
            shifts[l, j : j + 1, :] = row(11 + 2 * j, D)
        bout[l : l + 1, :] = row(15, D)
        bup[l : l + 1, :] = row(0, FF)
        bdown[l : l + 1, :] = row(17, D)


def body(
    inputs,
    lengths,
    gene_mask,
    out_grad,
    gain,
    bias,
    wqkv,
    wout,
    bout,
    feats,
    wup,
    bup,
    wdown,
    bdown,
):
    def flip(value):
        return jnp.swapaxes(value, -1, -2)

    streams_and_sums = layers(
        (
            flip(inputs),
            lengths,
            gene_mask,
            flip(out_grad),
            gain,
            bias,
            wqkv,
            flip(wout),
            bout,
            feats,
            wup,
            bup,
            flip(wdown),
            bdown,
        )
    )
    acts, sgrads, gains, shifts, qkv, out, dbout, up, dbup, down, dbdown = finish(*streams_and_sums)
    return (
        flip(acts)[None],
        flip(sgrads)[None],
        gains,
        shifts,
        qkv,
        flip(out),
        dbout,
        up,
        dbup,
        flip(down),
        dbdown,
    )


def solution(mesh):
    placed = (
        P("dp", None, None),
        P("dp"),
        P("dp", None),
        P("dp", None, None),
    ) + (P(),) * 10
    return jax.shard_map(
        body,
        mesh=mesh,
        in_specs=placed,
        out_specs=(P("section", "dp", None, None),) * 2 + (P(),) * 9,
        check_vma=False,
    )
```

time: 784 us -> 84.5 us (0.11); the launches traced: 771 us -> 84.4 us
  matrix products: 252 us -> 0 us
  local copies, waits for them, and re-layouts: 215 us -> 0 us
  waiting for transfers between devices: 115 us -> 0 us
  blocking collectives: 89.8 us -> 0 us
  Pallas kernels: 0 us -> 83.5 us
  other arithmetic: 57 us -> 0 us
  loops' own time: 16.6 us -> 0 us
  between operations: 15.8 us -> 0.82 us
  starting transfers between devices: 10.5 us -> 0 us
    dot_general x115 -> x0, matrix products: 252 us -> none  [the longest x20 66.5 us: feature_logits(): jnp.einsum('cnhe,ef->cnhf', vectors, random_map, preferred_element_type=j...]
    psum x1 -> x0, blocking collectives: 89.8 us -> none  [body(): lax.psum((slot_hot[..., None] * gain_grad, slot_hot[..., None] * shift_gr...]
    reshape x33 -> x0, local copies, waits for them, and re-layouts: 89.4 us -> none  [the longest x10 44 us: attend_forward(): projected.reshape(cell_count, slot_count, 3, HEADS, inner_width // HEADS)]
    pallas_call x0 -> x2, Pallas kernels: none -> 83.5 us  [the longest x1 79.5 us: layers(): pl.pallas_call(layers_kernel, out_shape=(pltpu.VMEM((8, D, SLOTS), F32),...]
    psum x1 -> x0, waiting for transfers between devices: 60.2 us -> none  [body(): lax.psum((slot_hot[..., None] * gain_grad, slot_hot[..., None] * shift_gr...]
    convert_element_type x25 -> x0, local copies, waits for them, and re-layouts: 55.5 us -> none  [the longest x10 40.1 us: attend_forward(): jnp.dot(normed_low, qkv_mats, preferred_element_type=jnp.float32)]
    ppermute x8 -> x0, waiting for transfers between devices: 54.4 us -> none  [from_behind(): return lax.ppermute(value, axis, pairs)]
    squeeze x8 -> x0, local copies, waits for them, and re-layouts: 18.7 us -> none  [the longest x5 16.1 us: attend_forward(): query, keys, values = (shaped[:, :, 0], shaped[:, :, 1], shaped[:, :, 2])]
  transfers between devices with their start and end apart: 9 -> 0, of which waited for: 9 -> 0; matrix products, arithmetic and copies ran while one was open for 4% -> 0% of each run, Pallas kernels for 0% -> 0%
where the time goes in v1:
time: 84.5 us; the launch traced here: 84.4 us
  Pallas kernels  83.5 us (99%)
    pallas_call x1, Pallas kernels, layers(): pl.pallas_call(layers_kernel, out_shape=(pltpu.VMEM((8, D, SLOTS), F32),...  79.5 us
    pallas_call x1, Pallas kernels, finish(): pl.pallas_call(finish_kernel, out_shape=(shape(8, D, SLOTS), shape(8, D,...  4.05 us

profile of v1, /device:TPU:1, one launch (start us, length us, event | category | flops | bytes accessed | tf_op | source)
XLA Modules:
  0.0 84.4 jit_solution(11199310257814726496)
XLA Ops:
  0.6 79.5 %layers.1 = (f32[8,200,128]{2,1,0:T(8,128)S(1)}, f32[8,200,128]{2,1,0:T(8,128)S(1)}, f32[14336,128]{1,0:T(8,128)S(1)}) custom-call(bf16[8,200,128]{2,1,0:T(8,128)(2,1)} %bitcast.15, s32[8]{0:T(128)} %lengths.1, s32[8,128]{1,0:T(8,128)} %gene_mask.1, f32[8,200,128]{2,1,0:T(8,128)} %bitcast.12, f32[2,2,200]{2,1,0:T(2,128)} %gain.1, f32[2,2,200]{2,1,0:T(2,128)} %bias.1, ...), custom_call_target="tpu_custom_call" | custom-call | tf_op jit(solution)/shard_map/layers/pallas_call | solution.py:478
  80.2 4.0 %finish.1 = (f32[8,200,128]{2,1,0:T(8,128)}, f32[8,200,128]{2,1,0:T(8,128)}, f32[2,2,200]{2,1,0:T(2,128)}, f32[2,2,200]{2,1,0:T(2,128)}, f32[2,200,1920]{2,1,0:T...) custom-call(f32[8,200,128]{2,1,0:T(8,128)S(1)} %get-tuple-element.25, ...), custom_call_target="tpu_custom_call" | custom-call | tf_op jit(solution)/shard_map/finish/pallas_call | solution.py:904

commit v2 on v1

--- a/solution.py
+++ b/solution.py
@@ -32,8 +32,10 @@
 TOTAL_BACK = S_NORM / Q_SCALE
 
 COL = 200
-EARLY = [("out", j) for j in range(5)] + [("up", j) for j in range(7)] + [("down", j) for j in range(7)]
-D_ROW, E_ROW, C_ROW, A_ROW, B_ROW, G_ROWS = 0, 2048, 3072, 7168, 11264, 14336
+QK = [("qkv", j) for j in range(10)]
+OUT_V = [("out", j) for j in range(5)] + [("qkv", j) for j in range(10, 15)]
+UP_DOWN = [("up", j) for j in range(7)] + [("down", j) for j in range(7)]
+D_ROW, E_ROW, C_ROW, A_ROW, F_ROW, B_ROW, G_ROWS = 0, 2048, 4096, 6912, 9728, 11776, 13824
 
 
 def place_columns():
@@ -45,19 +47,19 @@
             at += COL
         return at
 
-    qkv = [("qkv", j) for j in range(15)]
     ends = [
-        put(0, qkv[0:10], D_ROW) + 24,
-        put(0, qkv[10:], E_ROW),
-        put(0, EARLY, C_ROW),
-        put(1, EARLY, A_ROW),
-        put(1, qkv, B_ROW) + 24,
+        put(0, QK, D_ROW) + 24,
+        put(0, OUT_V, E_ROW),
+        put(0, UP_DOWN, C_ROW),
+        put(1, UP_DOWN, A_ROW),
+        put(1, OUT_V, F_ROW),
+        put(1, QK, B_ROW) + 24,
     ]
     return rows, ends
 
 
 ROWS, ENDS = place_columns()
-SMALL_ROW = (ENDS[0] - 24, ENDS[4] - 24)
+SMALL_ROW = (ENDS[0] - 24, ENDS[5] - 24)
 
 BF = jnp.bfloat16
 F32 = jnp.float32
@@ -141,7 +143,7 @@
         if end > start:
             g[start:end, :] = jnp.zeros((end - start, 128), F32)
 
-    for end, limit in zip(ENDS, (E_ROW, C_ROW, A_ROW, B_ROW, G_ROWS)):
+    for end, limit in zip(ENDS, (E_ROW, C_ROW, A_ROW, F_ROW, B_ROW, G_ROWS)):
         clear(end, limit)
     for l in range(LAYERS):
         clear(SMALL_ROW[l], SMALL_ROW[l] + 24)
@@ -198,6 +200,7 @@
     hop1,
     near1,
     t1,
+    hop2,
     near2,
     last,
     relay,
@@ -211,7 +214,7 @@
     greet(place)
     parts, before = {}, 0
     for name, t, axes, kind in PARTS:
-        bufs = (own, hop1, near1, t1, near2, last)
+        bufs = (own, hop1, near1, t1, hop2, near2, last)
         parts[name] = Part(place, wire, t, axes, kind, before, g, out, bufs)
         before += t
     act_stream = Streams(place, wire, acts, acts_out, relay.at[0])
@@ -462,13 +465,14 @@
         pltpu.VMEM((2 * LAYERS, 2, D, SLOTS), F32),
         pltpu.VMEM((2 * LAYERS, 2, D, SLOTS), F32),
         pltpu.VMEM((2 * LAYERS, rows, D), F32),
-        share(1024),
-        share(512),
+        share(256),
         share(128),
-        share(128, 3),
-        share(128),
+        share(32),
         share(32, 3),
-        share(32, 4),
+        share(32),
+        share(8),
+        share(8, 3),
+        share(8, 4),
         pltpu.VMEM((2, 2, D, SLOTS), F32),
         pltpu.SemaphoreType.DMA((2 + 4 * LAYERS,)),
         pltpu.SemaphoreType.DMA((SENDS,)),
@@ -480,7 +484,7 @@
         out_shape=(
             pltpu.VMEM((8, D, SLOTS), F32),
             pltpu.VMEM((8, D, SLOTS), F32),
-            pltpu.VMEM((1024 * SHARE, 128), F32),
+            pltpu.VMEM((256 * SHARE, 128), F32),
         ),
         in_specs=[hbm, smem, vmem, hbm, vmem, vmem, hbm, hbm, vmem, vmem, hbm, vmem, hbm, vmem],
         out_specs=(vmem, vmem, vmem),
@@ -495,29 +499,29 @@
 MESH = pl.DeviceIdType.MESH
 
 PARTS = (
-    ("D0", 1, "yzx", False),
-    ("D1", 1, "zxy", False),
-    ("E0", 1, "yxz", True),
-    ("C0", 3, "xyz", True),
-    ("C1", 1, "zxy", True),
-    ("A0", 4, "zyx", True),
-    ("B0", 3, "yxz", True),
+    ("D0", 5, "yxz", "rqw"),
+    ("D1", 3, "xyz", "rqw"),
+    ("E0", 8, "xyz", "rqw"),
+    ("C0", 11, "zyx", "rrw"),
+    ("A0", 11, "xzy", "rqb"),
+    ("F0", 8, "zyx", "rqw"),
+    ("B0", 8, "yxz", "rqb"),
 )
 SHARE = sum(part[1] for part in PARTS)
-SENDS = 20 * len(PARTS) + 12
+SENDS = 21 * len(PARTS) + 12
 
 DURING = (
-    {"pre": "C0 B0 C1", "k0": "A0", "k4": "E0", "back": "C0 C1 B0", "post": "D1 E0 D0"},
-    {"pre": "A0", "k0": "acts", "post": "B0 A0"},
+    {"mix1": "A0 F0", "mix2": "C0 B0", "q0": "A0 C0 B0 F0", "k4": "E0 A0", "back": "C0 B0", "post": "E0 D0 D1 A0 F0"},
+    {"mix2": "A0", "q3": "acts", "k0": "A0", "k4": "F0", "post": "B0"},
 )
 BEHIND = (
-    "A0", "C1", "D1", "C0", "D0", "B0", "E0", "A0",
-    "C0", "B0", "C1", "D0", "E0", "sg", "D1", "C0",
-    "A0", "C1", "E0", "D1", "B0", "D0", "A0", "C0",
-    "C1", "E0", "D1", "B0", "D0", "A0", "C0", "C1",
-    "E0", "D1", "B0", "D0", "C0", "E0", "A0", "C1",
-    "B0", "C0", "A0", "D1", "C1", "D0", "B0", "E0",
-    "C0", "D1", "C1", "D0", "E0",
+    "C0", "D0", "D1", "E0", "A0", "B0", "C0", "F0",
+    "D0", "D1", "C0", "E0", "D0", "sg", "D1", "F0",
+    "A0", "B0", "C0", "E0", "D0", "D1", "F0", "B0",
+    "C0", "A0", "E0", "D0", "C0", "D1", "B0", "F0",
+    "A0", "E0", "D0", "C0", "D1", "A0", "B0", "E0",
+    "D0", "F0", "D1", "B0", "C0", "F0", "D0", "E0",
+    "D1", "B0", "C0", "D0", "E0", "D1",
 )
 
 
@@ -534,6 +538,10 @@
 
         self.ahead, self.behind = 1 + 2 * self.core, 3 - 2 * self.core
         self.steps, self.peers = {}, {}
+        self.turns = {}
+        for axis, at in self.at.items():
+            odd = lax.rem(at, 2)
+            self.turns[axis] = (1 + 2 * odd, 3 - 2 * odd)
 
     def step(self, axis, by):
         key = axis, by if isinstance(by, int) else id(by)
@@ -645,11 +653,14 @@
         start = base + self.place.step(self.axis, by) * self.quarter
         return pl.ds(pl.multiple_of(start, 8), self.quarter)
 
-    def begin(self, block, near):
-        self.block, self.near, self.got = block, near, []
-
-    def send(self, by):
-        src, dst = self.block.at[self.rows(by)], self.near.at[by - 1]
+    def buffers(self, hop, near):
+        self.near, self.got = near, []
+
+    def order(self):
+        return (2, 1, 3)
+
+    def send(self, block, by):
+        src, dst = block.at[self.rows(by)], self.near.at[by - 1]
         self.got.append(self.wire.send(src, dst, self.place.peer(self.axis, by)))
 
     def result(self, block):
@@ -681,20 +692,23 @@
     def buffers(self, hop, near):
         self.hop, self.near = hop, near
 
+    def order(self):
+        return (2, self.behind)
+
+    def send(self, block, by):
+        src = block.at[self.rows(by)]
+        if by is self.behind:
+            self.got = [self.wire.send(src, self.near.at[1], self.to_behind)]
+        else:
+            self.far = self.wire.send(src, self.hop, self.to_ahead)
+
     def rows(self, by, base=0):
         start = base + self.place.step(self.axis, by) * self.quarter
         return pl.ds(pl.multiple_of(start, 8), self.quarter)
 
-    def send_far(self, block):
-        self.far = self.wire.send(block.at[self.rows(2)], self.hop, self.to_ahead)
-
-    def send_near(self, block):
-        src = block.at[self.rows(self.behind)]
-        self.got = [self.wire.send(src, self.near.at[1], self.to_behind)]
-
-    def send_sum(self, block):
+    def send_sum(self, block, more=0.0):
         self.far.wait_recv()
-        self.hop[...] = self.hop[...] + block[self.rows(self.ahead), :]
+        self.hop[...] = (self.hop[...] + block[self.rows(self.ahead), :]) + more
         self.got.append(self.wire.send(self.hop, self.near.at[0], self.to_ahead))
 
     def result(self, block):
@@ -716,53 +730,48 @@
     def arrivals(self):
         return zip(self.others, (self.ahead, 2))
 
+    def spread_end(self):
+        for copy in self.others:
+            copy.wait_recv()
+
 
 class Part:
-    def __init__(self, place, wire, tiles, axes, ring, before, g, out, bufs):
+    def __init__(self, place, wire, tiles, axes, kind, before, g, out, bufs):
         self.place, self.wire, self.axes, self.g, self.out = place, wire, axes, g, out
         t, b = tiles, before
         self.t, self.b = t, b
-        base, core = 1024 * b, place.core
-        self.mine = pl.multiple_of(base + core * (512 * t), 8)
-        self.other = pl.multiple_of(base + (1 - core) * (512 * t), 8)
-        self.at1 = self.mine + place.at[axes[0]] * (128 * t)
-        self.at2 = self.at1 + place.at[axes[1]] * (32 * t)
-        own, hop1, near1, t1, near2, last = bufs
+        base, core = 256 * b, place.core
+        self.mine = pl.multiple_of(base + core * (128 * t), 8)
+        self.other = pl.multiple_of(base + (1 - core) * (128 * t), 8)
+        self.at1 = self.mine + place.at[axes[0]] * (32 * t)
+        self.at2 = self.at1 + place.at[axes[1]] * (8 * t)
+        own, hop1, near1, t1, hop2, near2, last = bufs
         self.own_all = own
-        self.own = own.at[self.spot(512)]
-        self.near1 = near1.at[:, self.spot(128)]
-        self.t1 = t1.at[self.spot(128)]
-        self.near2 = near2.at[:, self.spot(32)]
-        self.last = last.at[:, self.spot(32)]
-        self.phase2 = Quarters(place, wire, axes[1], 32 * t)
+        self.own = own.at[self.spot(128)]
+        self.t1 = t1.at[self.spot(32)]
+        self.last = last.at[:, self.spot(8)]
+        self.phase1 = (Ring if kind[0] == "r" else Quarters)(place, wire, axes[0], 32 * t)
+        self.phase1.buffers(hop1.at[self.spot(32)], near1.at[:, self.spot(32)])
+        self.phase2 = (Ring if kind[1] == "r" else Quarters)(place, wire, axes[1], 8 * t)
+        self.phase2.buffers(hop2.at[self.spot(8)], near2.at[:, self.spot(8)])
+        self.whole = kind[2] == "w"
         self.at = 0
-        if ring:
-            self.phase1 = Ring(place, wire, axes[0], 128 * t)
-            self.phase1.buffers(hop1.at[self.spot(128)], self.near1)
-            self.steps = [
-                self.swap,
-                self.join_ring,
-                self.sums,
-                self.second,
-                self.third,
-                self.total,
-                self.back1,
-                self.back1_on,
-                self.give_rest,
-                self.taken,
-            ]
-        else:
-            self.phase1 = Quarters(place, wire, axes[0], 128 * t)
-            self.steps = [
-                self.swap,
-                self.join,
-                self.second,
-                self.third,
-                self.total,
-                self.back1,
-                self.give_rest,
-                self.taken,
-            ]
+        self.steps = [self.swap, self.join]
+        if kind[0] == "r":
+            self.steps.append(self.sums)
+        self.steps.append(self.second)
+        if kind[1] == "r":
+            self.steps.append(self.second_sums)
+        self.steps.append(self.third)
+        if not self.whole:
+            self.steps.append(self.third_again)
+        self.steps.append(self.total)
+        if kind[1] == "r":
+            self.steps.append(self.back2_on)
+        self.steps.append(self.back1)
+        if kind[0] == "r":
+            self.steps.append(self.back1_on)
+        self.steps += [self.give_rest, self.taken]
 
     def advance(self):
         self.steps[self.at]()
@@ -772,57 +781,71 @@
         return pl.ds(rows * self.b, rows * self.t)
 
     def swap(self):
-        src = self.g.at[pl.ds(self.other, 512 * self.t)]
+        src = self.g.at[pl.ds(self.other, 128 * self.t)]
         self.swapped = self.wire.send(src, self.own, self.place.peer("core", 1))
 
     def add_quarter(self, by):
-        rows = 128 * self.t
+        rows = 32 * self.t
         start = self.place.step(self.axes[0], by) * rows
-        to = pl.ds(pl.multiple_of(512 * self.b + start, 8), rows)
+        to = pl.ds(pl.multiple_of(128 * self.b + start, 8), rows)
         mine = pl.ds(pl.multiple_of(self.mine + start, 8), rows)
         self.own_all[to, :] = self.own_all[to, :] + self.g[mine, :]
 
     def join(self):
         self.swapped.wait_recv()
-        self.phase1.begin(self.own, self.near1)
-        for by in (2, 1, 3):
+        for by in self.phase1.order():
             self.add_quarter(by)
-            self.phase1.send(by)
-        self.add_quarter(0)
-
-    def join_ring(self):
-        self.swapped.wait_recv()
-        self.add_quarter(2)
-        self.phase1.send_far(self.own)
-        self.add_quarter(self.place.behind)
-        self.phase1.send_near(self.own)
-        self.add_quarter(self.place.ahead)
-        self.add_quarter(0)
+            self.phase1.send(self.own, by)
+
+    def rest(self, by):
+        start = self.place.step(self.axes[0], by) * (32 * self.t)
+        return self.g[pl.ds(pl.multiple_of(self.mine + start, 8), 32 * self.t), :]
 
     def sums(self):
-        self.phase1.send_sum(self.own)
+        self.phase1.send_sum(self.own, self.rest(self.place.ahead))
 
     def second(self):
-        self.t1[...] = self.phase1.result(self.own)
-        self.phase2.begin(self.t1, self.near2)
-        for by in (2, 1, 3):
-            self.phase2.send(by)
+        self.t1[...] = self.phase1.result(self.own) + self.rest(0)
+        for by in self.phase2.order():
+            self.phase2.send(self.t1, by)
+
+    def second_sums(self):
+        self.phase2.send_sum(self.t1)
 
     def third(self):
-        here = self.place.at[self.axes[2]]
-        self.last[here] = self.phase2.result(self.t1)
-        view = self.last.at[here]
-        self.thirds = [
-            self.wire.send(view, view, self.place.peer(self.axes[2], by)) for by in (2, 1, 3)
-        ]
+        axis = self.axes[2]
+        value = self.phase2.result(self.t1)
+        if self.whole:
+            here = self.place.at[axis]
+            self.last[here] = value
+            view = self.last.at[here]
+            self.thirds = [
+                self.wire.send(view, view, self.place.peer(axis, by)) for by in (2, 1, 3)
+            ]
+        else:
+            self.last[0] = value
+            to = self.place.peer(axis, self.place.turns[axis][0])
+            self.thirds = [self.wire.send(self.last.at[0], self.last.at[1], to)]
+
+    def third_again(self):
+        self.thirds[0].wait_recv()
+        self.last[2] = self.last[0] + self.last[1]
+        to = self.place.peer(self.axes[2], self.place.turns[self.axes[2]][1])
+        self.thirds = [self.wire.send(self.last.at[2], self.last.at[3], to)]
 
     def total(self):
         for copy in self.thirds:
             copy.wait_recv()
         z = self.last
-        rows = pl.ds(pl.multiple_of(self.at2, 8), 32 * self.t)
-        self.out[rows, :] = (z[0] + z[1]) + (z[2] + z[3])
+        rows = pl.ds(pl.multiple_of(self.at2, 8), 8 * self.t)
+        if self.whole:
+            self.out[rows, :] = (z[0] + z[1]) + (z[2] + z[3])
+        else:
+            self.out[rows, :] = z[2] + z[3]
         self.phase2.spread(self.out, self.at1)
+
+    def back2_on(self):
+        self.phase2.spread_on(self.out, self.at1)
 
     def back1(self):
         self.phase2.spread_end()

time: 84.5 us -> 84.5 us (level)
  no operation moved by 1% of the time
where the time goes in v2:
time: 84.5 us; the launch traced here: 84.3 us
  Pallas kernels  83.5 us (99%)
    pallas_call x1, Pallas kernels, layers(): pl.pallas_call(layers_kernel, out_shape=(pltpu.VMEM((8, D, SLOTS), F32),...  79.4 us
    pallas_call x1, Pallas kernels, finish(): pl.pallas_call(finish_kernel, out_shape=(shape(8, D, SLOTS), shape(8, D,...  4.05 us

profile of v2, /device:TPU:1, one launch (start us, length us, event | category | flops | bytes accessed | tf_op | source)
XLA Modules:
  0.0 84.3 jit_solution(6790592672896590202)
XLA Ops:
  0.6 79.4 %layers.1 = (f32[8,200,128]{2,1,0:T(8,128)S(1)}, f32[8,200,128]{2,1,0:T(8,128)S(1)}, f32[13824,128]{1,0:T(8,128)S(1)}) custom-call(bf16[8,200,128]{2,1,0:T(8,128)(2,1)} %bitcast.15, s32[8]{0:T(128)} %lengths.1, s32[8,128]{1,0:T(8,128)} %gene_mask.1, f32[8,200,128]{2,1,0:T(8,128)} %bitcast.12, f32[2,2,200]{2,1,0:T(2,128)} %gain.1, f32[2,2,200]{2,1,0:T(2,128)} %bias.1, ...), custom_call_target="tpu_custom_call" | custom-call | tf_op jit(solution)/shard_map/layers/pallas_call | solution.py:482
  80.1 4.0 %finish.1 = (f32[8,200,128]{2,1,0:T(8,128)}, f32[8,200,128]{2,1,0:T(8,128)}, f32[2,2,200]{2,1,0:T(2,128)}, f32[2,2,200]{2,1,0:T(2,128)}, f32[2,200,1920]{2,1,0:T...) custom-call(f32[8,200,128]{2,1,0:T(8,128)S(1)} %get-tuple-element.25, ...), custom_call_target="tpu_custom_call" | custom-call | tf_op jit(solution)/shard_map/finish/pallas_call | solution.py:927

commit v3 on v2

--- a/solution.py
+++ b/solution.py
@@ -77,6 +77,17 @@
     centered = rows - jnp.mean(rows, axis=-1, keepdims=True)
     inverse = lax.rsqrt(jnp.mean(centered * centered, axis=-1, keepdims=True) + EPSILON)
     return centered * inverse, inverse
+
+
+def normal_cdf(value, bell):
+    base = 1.0 + 0.3275911 * math.sqrt(0.5) * jnp.abs(value)
+    guess = pl.reciprocal(base, approx=True)
+    t = guess * (2.0 - base * guess)
+    poly = 1.061405429
+    for factor in (-1.453152027, 1.421413741, -0.284496736, 0.254829592):
+        poly = poly * t + factor
+    tail = 0.5 * poly * t * bell
+    return jnp.where(value < 0.0, tail, 1.0 - tail)
 
 
 def build_maps(feats_ref, fw):
@@ -311,10 +322,10 @@
         loads["up", l].wait()
         loads["down", l].wait()
         pre = mm(nb, wup[l]) + bup[l : l + 1]
-        cdf = 0.5 * (1.0 + lax.erf(pre * math.sqrt(0.5)))
+        bell = jnp.exp2(pre * pre * (-0.5 * LOG2E))
+        cdf = normal_cdf(pre, bell)
         hid[l] = (pre * cdf).astype(BF)
-        density = jnp.exp(-0.5 * pre * pre) * (1.0 / math.sqrt(2.0 * math.pi))
-        gp[l] = (cdf + pre * density).astype(BF)
+        gp[l] = (cdf + pre * bell * (1.0 / math.sqrt(2.0 * math.pi))).astype(BF)
         x[...] = x[...] + mm_t(hid[l], wdown[l]) + bdown[l : l + 1]
 
     def norm_backward(l, j, grad_normed):

time: 84.5 us -> 85.3 us (level)
    pallas_call x1, Pallas kernels: 79.4 us -> 80.3 us  [layers(): pl.pallas_call(layers_kernel, out_shape=(pltpu.VMEM((8, D, SLOTS), F32),...]
where the time goes in v3:
time: 85.3 us; the launch traced here: 85.2 us
  Pallas kernels  84.3 us (99%)
    pallas_call x1, Pallas kernels, layers(): pl.pallas_call(layers_kernel, out_shape=(pltpu.VMEM((8, D, SLOTS), F32),...  80.3 us
    pallas_call x1, Pallas kernels, finish(): pl.pallas_call(finish_kernel, out_shape=(shape(8, D, SLOTS), shape(8, D,...  4.05 us

profile of v3, /device:TPU:1, one launch (start us, length us, event | category | flops | bytes accessed | tf_op | source)
XLA Modules:
  0.0 85.2 jit_solution(1342339428174724444)
XLA Ops:
  0.6 80.3 %layers.1 = (f32[8,200,128]{2,1,0:T(8,128)S(1)}, f32[8,200,128]{2,1,0:T(8,128)S(1)}, f32[13824,128]{1,0:T(8,128)S(1)}) custom-call(bf16[8,200,128]{2,1,0:T(8,128)(2,1)} %bitcast.15, s32[8]{0:T(128)} %lengths.1, s32[8,128]{1,0:T(8,128)} %gene_mask.1, f32[8,200,128]{2,1,0:T(8,128)} %bitcast.12, f32[2,2,200]{2,1,0:T(2,128)} %gain.1, f32[2,2,200]{2,1,0:T(2,128)} %bias.1, ...), custom_call_target="tpu_custom_call" | custom-call | tf_op jit(solution)/shard_map/layers/pallas_call | solution.py:493
  81.0 4.0 %finish.1 = (f32[8,200,128]{2,1,0:T(8,128)}, f32[8,200,128]{2,1,0:T(8,128)}, f32[2,2,200]{2,1,0:T(2,128)}, f32[2,2,200]{2,1,0:T(2,128)}, f32[2,200,1920]{2,1,0:T...) custom-call(f32[8,200,128]{2,1,0:T(8,128)S(1)} %get-tuple-element.25, ...), custom_call_target="tpu_custom_call" | custom-call | tf_op jit(solution)/shard_map/finish/pallas_call | solution.py:938
